TPU v7x, 32 devices: a whole 2x2x4 slice. The times are simulated.
32 devices in a mesh: ctx: 2 (over x), head: 4 (over y, core), clip: 4 (over z).
Axes of the slice: x: 2, y: 2, z: 4, core: 2. Of those that a mesh axis runs over, the one named last changes fastest.
Arguments:
- queries: bfloat16 [4, 256, 2560], P('clip', 'ctx', 'head'), may hold values from -40 to 40
- key_states: bfloat16 [4, 256, 2560], P('clip', 'ctx', 'head'), may hold values from -40 to 40
- value_states: bfloat16 [4, 256, 2560], P('clip', 'ctx', 'head'), may hold values from -40 to 40
- layer_grad: bfloat16 [4, 256, 5120], P('clip', 'ctx'), may hold values from -6 to 6
- out_weight: bfloat16 [2560, 5120], P('head', 'clip'), may hold values from -0.125 to 0.125
- chosen: int32 [4, 4, 2], P('clip', 'ctx'), may hold values from 0 to 3, all different within a row
Outputs:
- attention: bfloat16 [4, 256, 2560], P('clip', 'ctx', 'head')
- query_grad: bfloat16 [4, 256, 2560], P('clip', 'ctx', 'head')
- key_grad: bfloat16 [4, 256, 2560], P('clip', 'ctx', 'head')
- value_grad: bfloat16 [4, 256, 2560], P('clip', 'ctx', 'head')
- weight_grad: bfloat16 [2560, 5120], P('head', 'clip')
Inputs may be any that keep to these rules, and one draw needn't show every extreme that they name: Each row names 2 different cubes of its clip; how often a key cube is chosen differs widely from cube to cube.
All inputs are finite; a program needn't handle non-finite values.
Results may differ from a plain program's by a relative error of at most 0.025.
Values may be sent and summed in bfloat16 or wider, within the bound.
A program may use at most 128 MiB of HBM per device.

v0:
```python
import jax
import jax.numpy as jnp
from jax import lax
from jax.sharding import PartitionSpec as P

HD = 128
CUBE = 64


def cube_means(blocks):
    grouped = blocks.astype(jnp.float32).reshape(-1, CUBE, blocks.shape[-1])
    return jnp.mean(grouped, axis=1).astype(jnp.bfloat16)


def by_heads(blocks):
    return blocks.reshape(blocks.shape[0], -1, HD)


def softmax_rows(scores):
    largest = jnp.max(scores, axis=-1, keepdims=True)
    expons = jnp.exp(scores - largest)
    return expons / jnp.sum(expons, axis=-1, keepdims=True)


def on_device(queries, key_states, value_states, layer_grad, out_weight, chosen):
    scaling = HD ** (-0.5)
    query_local = queries[0]
    key_local = key_states[0]
    value_local = value_states[0]
    layer_local = layer_grad[0]
    picked = chosen[0]
    tok_local, width = query_local.shape
    heads_here = width // HD
    cubes_local = tok_local // CUBE
    picks_each = picked.shape[1]
    key_whole, value_whole = (
        lax.all_gather(key_local, "ctx", axis=0, tiled=True),
        lax.all_gather(value_local, "ctx", axis=0, tiled=True),
    )
    tok_whole = key_whole.shape[0]
    cubes_whole = tok_whole // CUBE
    query_cube = cube_means(query_local)
    key_cube, value_cube = (
        lax.all_gather(cube_means(key_local), "ctx", axis=0, tiled=True),
        lax.all_gather(cube_means(value_local), "ctx", axis=0, tiled=True),
    )
    qcube_heads = by_heads(query_cube)
    kcube_heads = by_heads(key_cube)
    vcube_heads = by_heads(value_cube)
    coarse_scores = (
        jnp.einsum("ahd,bhd->hab", qcube_heads, kcube_heads, preferred_element_type=jnp.float32)
        * scaling
    )
    coarse_p = softmax_rows(coarse_scores)
    coarse_half = coarse_p.astype(jnp.bfloat16)
    coarse_out = jnp.einsum(
        "hab,bhd->ahd", coarse_half, vcube_heads, preferred_element_type=jnp.float32
    )
    key_cubes = key_whole.reshape(cubes_whole, CUBE, width)
    value_cubes = value_whole.reshape(cubes_whole, CUBE, width)
    key_pick = key_cubes[picked].reshape(cubes_local, picks_each * CUBE, heads_here, HD)
    value_pick = value_cubes[picked].reshape(cubes_local, picks_each * CUBE, heads_here, HD)
    query_blocks = query_local.reshape(cubes_local, CUBE, heads_here, HD)
    fine_scores = (
        jnp.einsum("cthd,ckhd->chtk", query_blocks, key_pick, preferred_element_type=jnp.float32)
        * scaling
    )
    fine_p = softmax_rows(fine_scores)
    fine_half = fine_p.astype(jnp.bfloat16)
    fine_out = jnp.einsum(
        "chtk,ckhd->cthd", fine_half, value_pick, preferred_element_type=jnp.float32
    )
    attention = (
        (fine_out + coarse_out[:, None, :, :]).astype(jnp.bfloat16).reshape(tok_local, width)
    )
    attn_grad = lax.dot_general(
        layer_local,
        lax.all_gather(out_weight, "clip", axis=1, tiled=True),
        (((1,), (1,)), ((), ())),
        preferred_element_type=jnp.float32,
    ).astype(jnp.bfloat16)
    grad_cube = jnp.sum(
        attn_grad.astype(jnp.float32).reshape(cubes_local, CUBE, width), axis=1
    ).astype(jnp.bfloat16)
    gcube_heads = by_heads(grad_cube)
    coarse_dp = jnp.einsum(
        "ahd,bhd->hab", gcube_heads, vcube_heads, preferred_element_type=jnp.float32
    )
    coarse_delta = jnp.sum(coarse_p * coarse_dp, axis=-1, keepdims=True)
    coarse_ds = (scaling * coarse_p * (coarse_dp - coarse_delta)).astype(jnp.bfloat16)
    coarse_dq = jnp.einsum(
        "hab,bhd->ahd", coarse_ds, kcube_heads, preferred_element_type=jnp.float32
    )
    coarse_dk = jnp.einsum(
        "hab,ahd->bhd", coarse_ds, qcube_heads, preferred_element_type=jnp.float32
    )
    coarse_dv = jnp.einsum(
        "hab,ahd->bhd", coarse_half, gcube_heads, preferred_element_type=jnp.float32
    )
    cube_terms = (
        jnp.concatenate(
            [coarse_dk.reshape(cubes_whole, width), coarse_dv.reshape(cubes_whole, width)], axis=1
        )
        / CUBE
    )
    grad_blocks = attn_grad.reshape(cubes_local, CUBE, heads_here, HD)
    fine_dp = jnp.einsum(
        "cthd,ckhd->chtk", grad_blocks, value_pick, preferred_element_type=jnp.float32
    )
    fine_delta = jnp.sum(fine_p * fine_dp, axis=-1, keepdims=True)
    fine_ds = (scaling * fine_p * (fine_dp - fine_delta)).astype(jnp.bfloat16)
    query_grad = jnp.einsum(
        "chtk,ckhd->cthd", fine_ds, key_pick, preferred_element_type=jnp.float32
    )
    query_grad = (query_grad + coarse_dq[:, None, :, :] / CUBE).astype(jnp.bfloat16)
    query_grad = query_grad.reshape(tok_local, width)
    key_picked = jnp.einsum(
        "chtk,cthd->ckhd", fine_ds, query_blocks, preferred_element_type=jnp.float32
    )
    value_picked = jnp.einsum(
        "chtk,cthd->ckhd", fine_half, grad_blocks, preferred_element_type=jnp.float32
    )
    flat_terms = jnp.concatenate(
        [
            key_picked.reshape(cubes_local, picks_each, CUBE, width),
            value_picked.reshape(cubes_local, picks_each, CUBE, width),
        ],
        axis=3,
    )
    flat_terms = flat_terms.reshape(cubes_local * picks_each, CUBE, 2 * width)
    picked_flat = picked.reshape(-1)
    running = jnp.broadcast_to(cube_terms[:, None, :], (cubes_whole, CUBE, 2 * width))
    running = running.at[picked_flat].add(flat_terms)
    summed = lax.psum_scatter(
        running.reshape(tok_whole, 2 * width).astype(jnp.bfloat16),
        "ctx",
        scatter_dimension=0,
        tiled=True,
    ).astype(jnp.float32)
    key_grad = summed[:, :width].astype(jnp.bfloat16)
    value_grad = summed[:, width:].astype(jnp.bfloat16)
    weight_term = lax.dot_general(
        attention, layer_local, (((0,), (0,)), ((), ())), preferred_element_type=jnp.float32
    )
    over_clips = lax.psum_scatter(
        weight_term.astype(jnp.bfloat16), "clip", scatter_dimension=1, tiled=True
    )
    over_groups = lax.psum(over_clips, "ctx").astype(jnp.float32)
    weight_grad = over_groups.astype(jnp.bfloat16)
    return (attention[None], query_grad[None], key_grad[None], value_grad[None], weight_grad)


def solution(mesh):
    placed = (
        P("clip", "ctx", "head"),
        P("clip", "ctx", "head"),
        P("clip", "ctx", "head"),
        P("clip", "ctx", None),
        P("head", "clip"),
        P("clip", "ctx", None),
    )
    return jax.shard_map(
        on_device,
        mesh=mesh,
        in_specs=placed,
        out_specs=(
            P("clip", "ctx", "head"),
            P("clip", "ctx", "head"),
            P("clip", "ctx", "head"),
            P("clip", "ctx", "head"),
            P("head", "clip"),
        ),
        check_vma=False,
    )
```

profile of v0, /device:TPU:0, one launch (start us, length us, event | category | flops | bytes accessed | tf_op | source)
XLA Modules:
  0.0 343.8 jit_solution(14520400882317885406)
XLA Ops:
  7.3 0.7 all-gather.6.cloned.1.call-update
  8.3 5.2 %all-gather.2 = bf16[2,2,640]{2,1,0:T(2,128)(2,1)S(1)} all-gather(bf16[1,2,640]{2,1,0:T(2,128)(2,1)S(1)} %fusion.31), channel_id=1, replica_groups=mesh['ctx'=2,'head'=4,'clip'=4] {'ctx'}, dimensions={0}, use_global_device_ids=true | all-gather | bytes 7680 | tf_op jit(solution)/shard_map/all_gather | solution.py:45
  13.6 4.3 %all-gather.3 = bf16[2,2,640]{2,1,0:T(2,128)(2,1)S(1)} all-gather(bf16[1,2,640]{2,1,0:T(2,128)(2,1)S(1)} %fusion.33), channel_id=1, replica_groups=mesh['ctx'=2,'head'=4,'clip'=4] {'ctx'}, dimensions={0}, use_global_device_ids=true | all-gather | bytes 7680 | tf_op jit(solution)/shard_map/all_gather | solution.py:44
  18.2 6.0 %all-gather.1 = bf16[1,256,640]{2,1,0:T(8,128)(2,1)S(1)} all-gather(bf16[1,128,640]{2,1,0:T(8,128)(2,1)S(1)} %copy-done.7), channel_id=3, replica_groups=mesh['ctx'=2,'head'=4,'clip'=4] {'ctx'}, dimensions={1}, use_global_device_ids=true | all-gather | bytes 491520 | tf_op jit(solution)/shard_map/all_gather | solution.py:37
  25.2 6.0 %all-gather = bf16[1,256,640]{2,1,0:T(8,128)(2,1)S(1)} all-gather(bf16[1,128,640]{2,1,0:T(8,128)(2,1)S(1)} %copy-done.8), channel_id=2, replica_groups=mesh['ctx'=2,'head'=4,'clip'=4] {'ctx'}, dimensions={1}, use_global_device_ids=true | all-gather | bytes 491520 | tf_op jit(solution)/shard_map/all_gather | solution.py:38
  32.8 1.7 fusion.47
  34.6 97.4 %all-gather.6.cloned.1.call-done = bf16[640,5120]{1,0:T(8,128)(2,1)} async-done(((bf16[640,1280]{1,0:T(8,128)(2,1)}), bf16[640,5120]{1,0:T(8,128)(2,1)}) %all-gather.6.cloned.1.call-update) | async-done | bytes 6553616 | tf_op jit(solution)/shard_map/all_gather | solution.py:78
  132.0 5.0 %bitcast_reduce_fusion = (bf16[2,640]{1,0:T(2,128)(2,1)S(1)}, bf16[128,640]{1,0:T(8,128)(2,1)S(1)}) fusion(bf16[640,5120]{1,0:T(8,128)(2,1)} %all-gather.6.cloned.1.call-done, bf16[1,128,5120]{2,1,0:T(8,128)(2,1)S(1)} %copy-done), kind=kOutput, calls=%fused_computation.45 | convolution fusion | flops 839023360 | bytes 8030720 | tf_op jit(solution)/shard_map/dot_general | solution.py:76
  137.0 1.3 multiply_reduce_fusion.1
  138.4 1.8 fusion.14
  140.3 1.0 copy.66
  141.3 0.7 copy-done.1
  142.0 4.6 %convolution_convert_fusion = bf16[640,5120]{1,0:T(8,128)(2,1)} fusion(bf16[1,128,5120]{2,1,0:T(8,128)(2,1)S(1)} %copy-done, bf16[16,8,5,128]{3,2,1,0:T(8,128)(2,1)S(1)} %bitcast.84), kind=kOutput, calls=%fused_computation.5 | convolution fusion | flops 842137600 | bytes 8028160 | tf_op jit(solution)/shard_map/dot_general | solution.py:142
  147.3 0.9 reshape.159
  148.2 1.4 multiply_reduce_fusion
  149.8 0.7 copy-done.3
  151.4 3.6 %convolution_bitcast_fusion = f32[2,128,5,128]{1,3,2,0:T(8,128)} fusion(bf16[2,64,5,128]{3,2,1,0:T(8,128)(2,1)} %reshape.159, f32[2,5,64]{2,1,0:T(8,128)S(1)} %get-tuple-element.14, f32[2,5,64,128]{3,2,1,0:T(8,128)} %copy-done.5), kind=kOutput, calls=%fused_computation.10 | convolution fusion | flops 21218048 | bytes 1149440 | tf_op jit(solution)/shard_map/chtk,cthd->ckhd/dot_general | solution.py:120
  155.0 1.5 copy.78
  156.5 1.1 concatenate.23
  157.6 0.9 convolution_bitcast_fusion.2
  158.4 0.8 multiply_convert_fusion.1
  159.2 0.9 convolution_bitcast_fusion.3
  160.1 2.3 pad_maximum_fusion
  162.9 2.5 scatter_fusion
  165.5 0.9 convert_element_type.116
  166.5 93.6 %reduce-scatter.5.cloned.1.call-done = bf16[640,1280]{1,0:T(8,128)(2,1)} async-done(((bf16[640,5120]{1,0:T(8,128)(2,1)}), bf16[640,1280]{1,0:T(8,128)(2,1)}) %reduce-scatter.5.cloned.1.call-update) | async-done | bytes 1638416 | tf_op jit(solution)/shard_map/reduce_scatter | solution.py:145
  260.1 0.9 broadcast_in_dim_reshape.6
  261.4 0.9 broadcast_in_dim_reshape.7
  262.3 17.1 %reduce-scatter.3.cloned.1.call-done = bf16[128,1280]{1,0:T(8,128)(2,1)} async-done(((bf16[256,1280]{1,0:T(8,128)(2,1)}), bf16[128,1280]{1,0:T(8,128)(2,1)}) %reduce-scatter.3.cloned.1.call-update) | async-done | bytes 327696 | tf_op jit(solution)/shard_map/reduce_scatter | solution.py:134
  279.4 1.7 slice_bitcast_fusion
  281.1 53.5 %all-reduce.2.cloned.1.call-done = bf16[640,1280]{1,0:T(8,128)(2,1)} async-done(((bf16[640,1280]{1,0:T(8,128)(2,1)}), bf16[640,1280]{1,0:T(8,128)(2,1)}) %all-reduce.2.cloned.1.call-update) | async-done | bytes 1638416 | tf_op jit(solution)/shard_map/psum | solution.py:148
  334.6 2.7 copy.119
  (66 shorter events, 6.3 us)
Async XLA Ops:
  7.2 124.8 %copy-start = (bf16[1,128,5120]{2,1,0:T(8,128)(2,1)S(1)}, bf16[1,128,5120]{2,1,0:T(8,128)(2,1)}, u32[]{:S(2)}) copy-start(bf16[1,128,5120]{2,1,0:T(8,128)(2,1)} %param.9) | copy-start | bytes 3932164
  7.2 0.8 copy-start.13
  7.2 1.0 copy-start.8
  7.2 6.3 %copy-start.7 = (bf16[1,128,640]{2,1,0:T(8,128)(2,1)S(1)}, bf16[1,128,640]{2,1,0:T(8,128)(2,1)}, u32[]{:S(2)}) copy-start(bf16[1,128,640]{2,1,0:T(8,128)(2,1)} %param.7) | copy-start | bytes 491524
  7.2 10.7 %copy-start.6 = (bf16[1,128,640]{2,1,0:T(8,128)(2,1)S(1)}, bf16[1,128,640]{2,1,0:T(8,128)(2,1)}, u32[]{:S(2)}) copy-start(bf16[1,128,640]{2,1,0:T(8,128)(2,1)} %param.6) | copy-start | bytes 491524
  7.2 124.8 %all-gather.6.cloned.1.call-start = ((), (), s32[]{:S(2)}) async-start(), calls=%async_computation.2 | async-start | bytes 8192000 | tf_op jit(solution)/shard_map/all_gather | solution.py:78
  8.0 252.1 %reduce-scatter.5.cloned.1.call-start = ((), (), s32[]{:S(2)}) async-start(), calls=%async_computation.4 | async-start | bytes 8192000 | tf_op jit(solution)/shard_map/reduce_scatter | solution.py:145
  32.2 104.8 %copy-start.11 = (f32[2,640]{1,0:T(2,128)}, f32[2,640]{1,0:T(2,128)S(1)}, u32[]{:S(2)}) copy-start(f32[2,640]{1,0:T(2,128)S(1)} %convert_reduce_fusion.1) | copy-start | bytes 15364
  32.8 105.6 %copy-start.5 = (f32[2,5,64,128]{3,2,1,0:T(8,128)}, f32[2,5,64,128]{3,2,1,0:T(8,128)S(1)}, u32[]{:S(2)}) copy-start(f32[2,5,64,128]{3,2,1,0:T(8,128)S(1)} %fusion.6) | copy-start | bytes 983044
  137.0 1.3 copy-start.12
  138.3 8.3 %copy-start.9 = (f32[5,2,4]{2,1,0:T(2,128)}, f32[5,2,4]{2,1,0:T(2,128)S(1)}, u32[]{:S(2)}) copy-start(f32[5,2,4]{2,1,0:T(2,128)S(1)} %get-tuple-element.6) | copy-start | bytes 484
  141.3 0.7 copy-start.1
  146.7 132.7 %reduce-scatter.3.cloned.1.call-start = ((), (), s32[]{:S(2)}) async-start(), calls=%async_computation.3 | async-start | bytes 983040 | tf_op jit(solution)/shard_map/reduce_scatter | solution.py:134
  149.8 0.7 copy-start.3
  155.0 2.6 copy-start.10
  162.4 0.6 copy-start.14
  166.4 93.7 %copy-start.2 = (bf16[2,64,5,128]{3,2,1,0:T(8,128)(2,1)S(1)}, bf16[2,64,5,128]{3,2,1,0:T(8,128)(2,1)}, u32[]{:S(2)}) copy-start(bf16[2,64,5,128]{3,2,1,0:T(8,128)(2,1)} %copy-done.1) | copy-start | bytes 491524
  166.4 94.7 %copy-start.4 = (bf16[2,5,64,128]{3,2,1,0:T(8,128)(2,1)S(1)}, bf16[2,5,64,128]{3,2,1,0:T(8,128)(2,1)}, u32[]{:S(2)}) copy-start(bf16[2,5,64,128]{3,2,1,0:T(8,128)(2,1)} %copy-done.3) | copy-start | bytes 491524
  166.4 168.2 %all-reduce.2.cloned.1.call-start = ((), (), s32[]{:S(2)}) async-start(), calls=%async_computation.5 | async-start | bytes 3276800 | tf_op jit(solution)/shard_map/psum | solution.py:148
Sparse Core Ops, SparseCore 0:
  9.6 122.3 all-gather.5
  146.8 113.1 reduce-scatter.4
  262.9 16.4 reduce-scatter.2
  281.6 52.9 all-reduce.1
where the time goes:
time: 344 us
  waiting for transfers between devices  262 us (76%)
  blocking collectives  21.6 us (6%)
  matrix products  20.8 us (6%)
  local copies, waits for them, and re-layouts  15.9 us (5%)
  between operations  14 us (4%)
  other arithmetic  9.1 us (3%)
    all_gather x1, waiting for transfers between devices, on_device(): lax.all_gather(out_weight, 'clip', axis=1, tiled=True)  97.4 us
    reduce_scatter x1, waiting for transfers between devices, on_device(): lax.psum_scatter(weight_term.astype(jnp.bfloat16), 'clip', scatter_dimens...  93.6 us
    psum x1, waiting for transfers between devices, on_device(): over_groups = lax.psum(over_clips, 'ctx').astype(jnp.float32)  53.5 us
    reduce_scatter x1, waiting for transfers between devices, on_device(): lax.psum_scatter(running.reshape(tok_whole, 2 * width).astype(jnp.bfloat1...  17.1 us
  transfers between devices with their start and end apart: 4, of which 4 were waited for; matrix products, arithmetic and copies ran while one was open for 8% of the time, Pallas kernels for 0%

commit v1 on v0

--- a/solution.py
+++ b/solution.py
@@ -33,17 +33,23 @@
     heads_here = width // HD
     cubes_local = tok_local // CUBE
     picks_each = picked.shape[1]
-    key_whole, value_whole = (
-        lax.all_gather(key_local, "ctx", axis=0, tiled=True),
-        lax.all_gather(value_local, "ctx", axis=0, tiled=True),
+    kv_whole = lax.all_gather(
+        jnp.concatenate([key_local, value_local], axis=1), "ctx", axis=0, tiled=True
     )
+    key_whole, value_whole = kv_whole[:, :width], kv_whole[:, width:]
+    columns = lax.all_to_all(layer_local, "clip", split_axis=1, concat_axis=0, tiled=True)
+    grad_parts = lax.dot_general(
+        columns, out_weight, (((1,), (1,)), ((), ())), preferred_element_type=jnp.float32
+    ).astype(jnp.bfloat16)
+    grad_parts = lax.all_to_all(
+        grad_parts.reshape(-1, tok_local, width), "clip", split_axis=0, concat_axis=0, tiled=True
+    )
+    attn_grad = jnp.sum(grad_parts.astype(jnp.float32), axis=0).astype(jnp.bfloat16)
+    columns_whole = lax.all_gather(columns, "ctx", axis=0, tiled=True)
     tok_whole = key_whole.shape[0]
     cubes_whole = tok_whole // CUBE
     query_cube = cube_means(query_local)
-    key_cube, value_cube = (
-        lax.all_gather(cube_means(key_local), "ctx", axis=0, tiled=True),
-        lax.all_gather(cube_means(value_local), "ctx", axis=0, tiled=True),
-    )
+    key_cube, value_cube = cube_means(key_whole), cube_means(value_whole)
     qcube_heads = by_heads(query_cube)
     kcube_heads = by_heads(key_cube)
     vcube_heads = by_heads(value_cube)
@@ -73,12 +79,7 @@
     attention = (
         (fine_out + coarse_out[:, None, :, :]).astype(jnp.bfloat16).reshape(tok_local, width)
     )
-    attn_grad = lax.dot_general(
-        layer_local,
-        lax.all_gather(out_weight, "clip", axis=1, tiled=True),
-        (((1,), (1,)), ((), ())),
-        preferred_element_type=jnp.float32,
-    ).astype(jnp.bfloat16)
+    attention_whole = lax.all_gather(attention, ("ctx", "clip"), axis=0, tiled=True)
     grad_cube = jnp.sum(
         attn_grad.astype(jnp.float32).reshape(cubes_local, CUBE, width), axis=1
     ).astype(jnp.bfloat16)
@@ -139,14 +140,9 @@
     ).astype(jnp.float32)
     key_grad = summed[:, :width].astype(jnp.bfloat16)
     value_grad = summed[:, width:].astype(jnp.bfloat16)
-    weight_term = lax.dot_general(
-        attention, layer_local, (((0,), (0,)), ((), ())), preferred_element_type=jnp.float32
-    )
-    over_clips = lax.psum_scatter(
-        weight_term.astype(jnp.bfloat16), "clip", scatter_dimension=1, tiled=True
-    )
-    over_groups = lax.psum(over_clips, "ctx").astype(jnp.float32)
-    weight_grad = over_groups.astype(jnp.bfloat16)
+    weight_grad = lax.dot_general(
+        attention_whole, columns_whole, (((0,), (0,)), ((), ())), preferred_element_type=jnp.float32
+    ).astype(jnp.bfloat16)
     return (attention[None], query_grad[None], key_grad[None], value_grad[None], weight_grad)
 
 

time: 344 us -> 203 us (0.59)
  waiting for transfers between devices: 262 us -> 123 us
  blocking collectives: 21.6 us -> 9.85 us
  starting transfers between devices: 0.16 us -> 10.2 us
  matrix products: 20.8 us -> 16.4 us
  local copies, waits for them, and re-layouts: 15.9 us -> 20.2 us
    reduce_scatter x1 -> x0, waiting for transfers between devices: 93.6 us -> none  [on_device(): lax.psum_scatter(weight_term.astype(jnp.bfloat16), 'clip', scatter_dimens...]
    psum x1 -> x0, waiting for transfers between devices: 53.5 us -> none  [on_device(): over_groups = lax.psum(over_clips, 'ctx').astype(jnp.float32)]
    all_to_all x0 -> x2, waiting for transfers between devices: none -> 29.9 us  [the longest x1 19.4 us: on_device(): lax.all_to_all(layer_local, 'clip', split_axis=1, concat_axis=0, tiled=True)]
    all_gather x1 -> x2, waiting for transfers between devices: 97.4 us -> 83.4 us  [the longest x1 44.4 us: on_device(): lax.all_gather(attention, ('ctx', 'clip'), axis=0, tiled=True)]
    all_gather x4 -> x1, blocking collectives: 21.6 us -> 9.85 us  [on_device(): lax.all_gather(jnp.concatenate([key_local, value_local], axis=1), 'ctx',...]
    all_to_all x0 -> x2, starting transfers between devices: none -> 10.1 us  [the longest x1 6.45 us: on_device(): lax.all_to_all(layer_local, 'clip', split_axis=1, concat_axis=0, tiled=True)]
    reduce_scatter x1, waiting for transfers between devices: 17.1 us -> 8.95 us  [on_device(): lax.psum_scatter(running.reshape(tok_whole, 2 * width).astype(jnp.bfloat1...]
  transfers between devices with their start and end apart: 4 -> 5, of which waited for: 4 -> 5; matrix products, arithmetic and copies ran while one was open for 8% -> 8% of each run, Pallas kernels for 0% -> 0%
where the time goes in v1:
time: 203 us; the launch traced here: 202 us
  waiting for transfers between devices  123 us (61%)
  local copies, waits for them, and re-layouts  20.2 us (10%)
  matrix products  16.4 us (8%)
  between operations  14 us (7%)
  starting transfers between devices  10.2 us (5%)
  blocking collectives  9.85 us (5%)
  other arithmetic  8.44 us (4%)
    all_gather x1, waiting for transfers between devices, on_device(): lax.all_gather(attention, ('ctx', 'clip'), axis=0, tiled=True)  44.4 us
    all_gather x1, waiting for transfers between devices, on_device(): columns_whole = lax.all_gather(columns, 'ctx', axis=0, tiled=True)  39 us
    all_to_all x1, waiting for transfers between devices, on_device(): lax.all_to_all(layer_local, 'clip', split_axis=1, concat_axis=0, tiled=True)  19.4 us
    all_to_all x1, waiting for transfers between devices, on_device(): lax.all_to_all(grad_parts.reshape(-1, tok_local, width), 'clip', split_ax...  10.5 us
    all_gather x1, blocking collectives, on_device(): lax.all_gather(jnp.concatenate([key_local, value_local], axis=1), 'ctx',...  9.85 us
    reduce_scatter x1, waiting for transfers between devices, on_device(): lax.psum_scatter(running.reshape(tok_whole, 2 * width).astype(jnp.bfloat1...  8.95 us
    all_to_all x1, starting transfers between devices, on_device(): lax.all_to_all(layer_local, 'clip', split_axis=1, concat_axis=0, tiled=True)  6.45 us
    dot_general x1, matrix products, on_device(): lax.dot_general(attention_whole, columns_whole, (((0,), (0,)), ((), ())),...  5.21 us
  transfers between devices with their start and end apart: 5, of which 5 were waited for; matrix products, arithmetic and copies ran while one was open for 8% of the time, Pallas kernels for 0%

profile of v1, /device:TPU:0, one launch (start us, length us, event | category | flops | bytes accessed | tf_op | source)
XLA Modules:
  0.0 202.0 jit_solution(9501889572045646674)
XLA Ops:
  7.2 2.5 %copy.35 = bf16[1,128,5120]{1,2,0:T(8,128)(2,1)} copy(bf16[1,128,5120]{2,1,0:T(8,128)(2,1)} %param.9) | data formatting | bytes 2621440 | tf_op args[3]
  9.7 6.4 %all-to-all-start = ((bf16[128,4,1280]{0,2,1:T(8,128)(2,1)}), bf16[128,4,1280]{0,2,1:T(8,128)(2,1)S(1)}, u32[]{:S(2)}, u32[]{:S(2)}) async-start(bf16[128,4,1280]{0,2,1:T(8,128)(2,1)} %bitcast.91), calls=%async_computation | async-start | bytes 2621440 | tf_op jit(solution)/shard_map/all_to_all | solution.py:40
  16.3 1.0 pad_maximum_fusion.1
  17.3 9.8 %all_gather.9 = bf16[256,1280]{1,0:T(8,128)(2,1)S(1)} all-gather(bf16[128,1280]{1,0:T(8,128)(2,1)S(1)} %pad_maximum_fusion.1), channel_id=1, replica_groups=mesh['ctx'=2,'head'=4,'clip'=4] {'ctx'}, dimensions={0}, use_global_device_ids=true | all-gather | bytes 983040 | tf_op jit(solution)/shard_map/all_gather | solution.py:36
  27.3 0.8 fusion.42
  28.1 19.4 %all-to-all-done = bf16[128,4,1280]{0,2,1:T(8,128)(2,1)S(1)} async-done(((bf16[128,4,1280]{0,2,1:T(8,128)(2,1)}), bf16[128,4,1280]{0,2,1:T(8,128)(2,1)S(1)}, u32[]{:S(2)}, u32[]{:S(2)}) %all-to-all-start) | async-done | bytes 1310752 | tf_op jit(solution)/shard_map/all_to_all | solution.py:40
  47.5 1.1 copy-done.2
  48.6 1.6 copy.36
  50.2 2.1 %convolution_convert_fusion.1 = bf16[512,640]{1,0:T(8,128)(2,1)} fusion(bf16[512,1280]{1,0:T(8,128)(2,1)S(1)} %bitcast.88, bf16[640,1280]{1,0:T(8,128)(2,1)S(1)} %copy-done), kind=kOutput, calls=%fused_computation.6 | convolution fusion | flops 839188480 | bytes 3604480 | tf_op jit(solution)/shard_map/dot_general | solution.py:41
  52.3 3.6 %all-to-all-start.1 = ((bf16[4,128,640]{2,1,0:T(8,128)(2,1)}), bf16[4,128,640]{2,1,0:T(8,128)(2,1)S(1)}, u32[]{:S(2)}, u32[]{:S(2)}) async-start(bf16[4,128,640]{2,1,0:T(8,128)(2,1)} %bitcast.96), calls=%async_computation.1 | async-start | bytes 1310720 | tf_op jit(solution)/shard_map/all_to_all | solution.py:44
  56.2 1.3 gather_fusion
  57.5 2.1 %reshape.163 = bf16[2,128,5,128]{3,2,1,0:T(8,128)(2,1)} reshape(bf16[4,64,640]{2,1,0:T(8,128)(2,1)} %gather_fusion) | data formatting | bytes 655360 | tf_op jit(solution)/shard_map/reshape | solution.py:68
  61.3 0.9 fusion.44
  62.2 10.5 %all-to-all-done.1 = bf16[4,128,640]{2,1,0:T(8,128)(2,1)S(1)} async-done(((bf16[4,128,640]{2,1,0:T(8,128)(2,1)}), bf16[4,128,640]{2,1,0:T(8,128)(2,1)S(1)}, u32[]{:S(2)}, u32[]{:S(2)}) %all-to-all-start.1) | async-done | bytes 655392 | tf_op jit(solution)/shard_map/all_to_all | solution.py:44
  73.7 3.3 %convolution_bitcast_fusion = f32[2,128,5,128]{1,3,2,0:T(8,128)} fusion(bf16[2,64,5,128]{3,2,1,0:T(8,128)(2,1)S(1)} %reshape.169, f32[2,5,64]{2,1,0:T(8,128)S(1)} %get-tuple-element.16, f32[2,5,64,128]{3,2,1,0:T(8,128)} %copy-done.6), kind=kOutput, calls=%fused_computation.8 | convolution fusion | flops 21218048 | bytes 1149440 | tf_op jit(solution)/shard_map/chtk,cthd->ckhd/dot_general | solution.py:121
  77.0 1.5 copy.45
  78.5 1.0 concatenate.27
  79.5 1.7 multiply_reduce_fusion
  82.8 1.0 concatenate.26
  83.8 2.5 %pad_maximum_fusion = f32[4,64,1280]{2,1,0:T(8,128)} fusion(f32[4,64,640]{2,1,0:T(8,128)} %concatenate.27, f32[4,64,640]{2,1,0:T(8,128)} %concatenate.26), kind=kLoop, calls=%fused_computation.7 | loop fusion | flops 327680 | bytes 2621440 | tf_op jit(solution)/shard_map/concatenate | solution.py:124
  86.4 2.5 %scatter_fusion = f32[4,64,1280]{2,1,0:T(8,128)S(1)} fusion(f32[4,64,1280]{2,1,0:T(8,128)S(1)} %broadcast_in_dim.6, s32[4]{0:T(128)S(1)} %fusion.31, f32[4,64,1280]{2,1,0:T(8,128)} %pad_maximum_fusion), kind=kCustom, calls=%fused_computation.2 | custom fusion | flops 327680 | bytes 3932176 | tf_op jit(solution)/shard_map/scatter-add | solution.py:134
  88.9 0.9 convert_element_type.110
  89.9 0.7 all-gather.5.cloned.1.call-update
  90.9 2.2 %fusion.8 = bf16[2,64,5,128]{3,1,2,0:T(8,128)(2,1)S(1)} fusion(bf16[2,128,5,128]{3,2,1,0:T(8,128)(2,1)S(1)} %copy-done.9, f32[2,5,128]{2,1,0:T(8,128)S(1)} %copy.33, f32[2,5,64]{2,1,0:T(8,128)S(1)} %get-tuple-element.16, f32[2,5,64,128]{3,2,1,0:T(8,128)} %copy-done.6), kind=kOutput, calls=%fused_computation.19 | convolution fusion | flops 21381888 | bytes 826880 | tf_op jit(solution)/shard_map/chtk,ckhd->cthd/dot_general | solution.py:76
  93.2 0.7 copy.69
  94.0 0.9 broadcast_in_dim_reshape.6
  95.3 0.9 broadcast_in_dim_reshape.7
  96.2 8.9 %reduce-scatter.2.cloned.1.call-done = bf16[128,1280]{1,0:T(8,128)(2,1)} async-done(((bf16[256,1280]{1,0:T(8,128)(2,1)}), bf16[128,1280]{1,0:T(8,128)(2,1)}) %reduce-scatter.2.cloned.1.call-update) | async-done | bytes 327696 | tf_op jit(solution)/shard_map/reduce_scatter | solution.py:135
  105.2 1.7 slice_bitcast_fusion
  106.9 39.0 %all-gather.5.cloned.1.call-done = bf16[1024,1280]{1,0:T(8,128)(2,1)} async-done(((bf16[512,1280]{1,0:T(8,128)(2,1)}), bf16[1024,1280]{1,0:T(8,128)(2,1)}) %all-gather.5.cloned.1.call-update) | async-done | bytes 2621456 | tf_op jit(solution)/shard_map/all_gather | solution.py:48
  145.8 44.4 %all-gather.3.cloned.1.call-done = bf16[1024,640]{1,0:T(8,128)(2,1)} async-done(((bf16[128,640]{1,0:T(8,128)(2,1)}), bf16[1024,640]{1,0:T(8,128)(2,1)}) %all-gather.3.cloned.1.call-update) | async-done | bytes 1310736 | tf_op jit(solution)/shard_map/all_gather | solution.py:82
  190.3 5.2 %convolution_convert_fusion = bf16[640,1280]{1,0:T(8,128)(2,1)} fusion(bf16[1024,640]{1,0:T(8,128)(2,1)} %all-gather.3.cloned.1.call-done, bf16[1024,1280]{1,0:T(8,128)(2,1)} %all-gather.5.cloned.1.call-done), kind=kOutput, calls=%fused_computation.5 | convolution fusion | flops 1678540800 | bytes 5570560 | tf_op jit(solution)/shard_map/dot_general | solution.py:143
  (59 shorter events, 5.9 us)
Async XLA Ops:
  7.2 43.0 %copy-start = (bf16[640,1280]{1,0:T(8,128)(2,1)S(1)}, bf16[640,1280]{1,0:T(8,128)(2,1)}, u32[]{:S(2)}) copy-start(bf16[640,1280]{1,0:T(8,128)(2,1)} %param.10) | copy-start | bytes 4915204
  9.7 6.5 %copy-start.11 = (s32[1,2,2]{2,1,0:T(2,128)S(1)}, s32[1,2,2]{2,1,0:T(2,128)}, u32[]{:S(2)}) copy-start(s32[1,2,2]{2,1,0:T(2,128)} %param.11) | copy-start | bytes 52
  9.7 6.5 %copy-start.8 = (bf16[1,128,640]{2,1,0:T(8,128)(2,1)S(1)}, bf16[1,128,640]{2,1,0:T(8,128)(2,1)}, u32[]{:S(2)}) copy-start(bf16[1,128,640]{2,1,0:T(8,128)(2,1)} %param.6) | copy-start | bytes 491524
  9.7 37.8 %all-to-all-start = ((bf16[128,4,1280]{0,2,1:T(8,128)(2,1)}), bf16[128,4,1280]{0,2,1:T(8,128)(2,1)S(1)}, u32[]{:S(2)}, u32[]{:S(2)}) async-start(bf16[128,4,1280]{0,2,1:T(8,128)(2,1)} %bitcast.91), calls=%async_computation | async-start | bytes 2621440 | tf_op jit(solution)/shard_map/all_to_all | solution.py:40
  47.5 1.1 copy-start.2
  50.2 2.1 %copy-start.1 = (bf16[4,128,1280]{2,1,0:T(8,128)(2,1)}, bf16[4,128,1280]{2,1,0:T(8,128)(2,1)S(1)}, u32[]{:S(2)}) copy-start(bf16[4,128,1280]{2,1,0:T(8,128)(2,1)S(1)} %copy.36) | copy-start | bytes 3932164
  52.3 4.0 %copy-start.5 = (bf16[256,640]{1,0:T(8,128)(2,1)S(1)}, bf16[256,640]{1,0:T(8,128)(2,1)}, u32[]{:S(2)}) copy-start(bf16[256,640]{1,0:T(8,128)(2,1)} %get-tuple-element.10) | copy-start | bytes 983044
  52.3 20.4 %all-to-all-start.1 = ((bf16[4,128,640]{2,1,0:T(8,128)(2,1)}), bf16[4,128,640]{2,1,0:T(8,128)(2,1)S(1)}, u32[]{:S(2)}, u32[]{:S(2)}) async-start(bf16[4,128,640]{2,1,0:T(8,128)(2,1)} %bitcast.96), calls=%async_computation.1 | async-start | bytes 1310720 | tf_op jit(solution)/shard_map/all_to_all | solution.py:44
  55.9 49.3 %reduce-scatter.2.cloned.1.call-start = ((), (), s32[]{:S(2)}) async-start(), calls=%async_computation.3 | async-start | bytes 983040 | tf_op jit(solution)/shard_map/reduce_scatter | solution.py:135
  61.3 0.9 copy-start.6
  73.0 0.7 copy-start.10
  79.5 1.7 copy-start.7
  81.4 0.7 copy-start.3
  89.8 1.0 copy-start.9
  89.8 56.0 %all-gather.5.cloned.1.call-start = ((), (), s32[]{:S(2)}) async-start(), calls=%async_computation.5 | async-start | bytes 3932160 | tf_op jit(solution)/shard_map/all_gather | solution.py:48
  90.6 99.7 %all-gather.3.cloned.1.call-start = ((), (), s32[]{:S(2)}) async-start(), calls=%async_computation.4 | async-start | bytes 1474560 | tf_op jit(solution)/shard_map/all_gather | solution.py:82
  90.9 4.1 %copy-start.4 = (bf16[2,5,64,128]{3,2,1,0:T(8,128)(2,1)S(1)}, bf16[2,5,64,128]{3,2,1,0:T(8,128)(2,1)}, u32[]{:S(2)}) copy-start(bf16[2,5,64,128]{3,2,1,0:T(8,128)(2,1)} %copy-done.3) | copy-start | bytes 491524
Sparse Core Ops, SparseCore 0:
  90.0 15.1 reduce-scatter.1
  106.8 39.0 all-gather.4
  148.2 42.0 all-gather.2

commit v2 on v1

--- a/solution.py
+++ b/solution.py
@@ -1,6 +1,10 @@
+import functools
+
 import jax
 import jax.numpy as jnp
 from jax import lax
+from jax.experimental import pallas as pl
+from jax.experimental.pallas import tpu as pltpu
 from jax.sharding import PartitionSpec as P
 
 HD = 128
@@ -145,8 +149,294 @@
     ).astype(jnp.bfloat16)
     return (attention[None], query_grad[None], key_grad[None], value_grad[None], weight_grad)
 
+ROWS = 16
+LOW = -1e30
+
+
+def dot_nt(a, b):
+    return lax.dot_general(a, b, (((1,), (1,)), ((), ())), preferred_element_type=jnp.float32)
+
+
+def dot_nn(a, b):
+    return lax.dot_general(a, b, (((1,), (0,)), ((), ())), preferred_element_type=jnp.float32)
+
+
+def dot_tn(a, b):
+    return lax.dot_general(a, b, (((0,), (0,)), ((), ())), preferred_element_type=jnp.float32)
+
+
+def cube_rows(blocks, factor):
+    at_row = lax.broadcasted_iota(jnp.int32, (ROWS, blocks.shape[1]), 0)
+    rows = jnp.zeros((ROWS, blocks.shape[1]), jnp.float32)
+    for cube in range(blocks.shape[0] // CUBE):
+        part = blocks[cube * CUBE : (cube + 1) * CUBE].astype(jnp.float32)
+        total = jnp.sum(part, axis=0, keepdims=True) * factor
+        rows = jnp.where(at_row == cube, total, rows)
+    return rows.astype(jnp.bfloat16)
+
+
+def over_tokens(rows, cubes):
+    return jnp.concatenate(
+        [jnp.broadcast_to(rows[cube : cube + 1], (CUBE, rows.shape[1])) for cube in range(cubes)],
+        axis=0,
+    )
+
+
+def pair_kernel(
+    n_clip, n_head, chosen, query, key, value, layer, weight,
+    attention, query_grad, key_grad, value_grad, weight_grad,
+    keys, values, columns, held_weight, fine, coarse, turned,
+    partial, partial_in, grad, terms, terms_in,
+    kv_sem, deal_sem, share_sem, across_sem, share_far_sem, part_sem, turn_sem, turn_far_sem,
+    term_sem, local_sem,
+):
+    scaling = HD ** (-0.5)
+    tokens, width = query.shape
+    cols = weight.shape[1]
+    heads = width // HD
+    cubes = tokens // CUBE
+    cubes_whole = 2 * cubes
+    quarter = tokens // n_head
+    x, h, z = lax.axis_index("ctx"), lax.axis_index("head"), lax.axis_index("clip")
+    other = 1 - x
+    my_rows = pl.ds(pl.multiple_of(h * quarter, quarter), quarter)
+
+    def to_clip(step):
+        return {"clip": lax.rem(z + step, n_clip)}
+
+    def from_clip(step):
+        return lax.rem(z + n_clip - step, n_clip)
+
+    def to_head(step):
+        return {"head": lax.rem(h + step, n_head)}
+
+    def column_block(clip):
+        return pl.ds(pl.multiple_of(clip * cols, cols), cols)
+
+    def slot(ctx, clip):
+        return pl.ds(pl.multiple_of((ctx * n_clip + clip) * tokens, tokens), tokens)
+
+    sent = []
+
+    def send(src, dst, sems, index, device):
+        copy = pltpu.make_async_remote_copy(
+            src_ref=src, dst_ref=dst,
+            send_sem=sems.at[(0,) + index], recv_sem=sems.at[(1,) + index],
+            device_id=device, device_id_type=pl.DeviceIdType.MESH,
+        )
+        copy.start()
+        sent.append(copy)
+        return copy
+
+    weight_copy = pltpu.make_async_copy(weight, held_weight, local_sem.at[0])
+    weight_copy.start()
+    layer_copy = pltpu.make_async_copy(
+        layer.at[:, column_block(z)], columns.at[x, z], local_sem.at[1]
+    )
+    layer_copy.start()
+
+    barrier = pltpu.get_barrier_semaphore()
+    partners = [{"ctx": other}]
+    partners += [to_clip(step) for step in range(1, n_clip)]
+    partners += [to_head(step) for step in range(1, n_head)]
+    for partner in partners:
+        pl.semaphore_signal(barrier, inc=1, device_id=partner, device_id_type=pl.DeviceIdType.MESH)
+    pl.semaphore_wait(barrier, len(partners))
+
+    mine = pl.ds(pl.multiple_of(x * tokens, tokens), tokens)
+    key_copy = send(key, keys.at[mine], kv_sem, (0,), {"ctx": other})
+    value_copy = send(value, values.at[mine], kv_sem, (1,), {"ctx": other})
+    deals = [None]
+    for step in range(1, n_clip):
+        deals.append(
+            send(
+                layer.at[my_rows, column_block(lax.rem(z + step, n_clip))],
+                columns.at[x, z, my_rows], deal_sem, (step,), to_clip(step),
+            )
+        )
+    across = [
+        send(
+            layer.at[my_rows, column_block(z)], columns.at[x, z, my_rows],
+            across_sem, (0,), {"ctx": other},
+        )
+    ]
+    keys[mine, :] = key[...]
+    values[mine, :] = value[...]
+    query_cube = cube_rows(query[...], 1.0 / CUBE)
+    column_cube = lax.broadcasted_iota(jnp.int32, (1, cubes_whole * CUBE), 1) // CUBE
+    allowed = []
+    for cube in range(cubes):
+        hit = column_cube == chosen[cube, 0]
+        for pick in range(1, chosen.shape[1]):
+            hit = hit | (column_cube == chosen[cube, pick])
+        allowed.append(jnp.broadcast_to(hit.astype(jnp.float32), (CUBE, cubes_whole * CUBE)))
+    allowed = jnp.concatenate(allowed, axis=0) > 0.5
+    real = lax.broadcasted_iota(jnp.int32, (ROWS, ROWS), 1) < cubes_whole
+
+    shares = [None]
+
+    def pass_on(step):
+        deals[step].wait_recv()
+        piece = columns.at[x, from_clip(step), my_rows]
+        shares.append(
+            [send(piece, piece, share_sem, (step, turn), to_head(turn)) for turn in range(1, n_head)]
+        )
+        across.append(send(piece, piece, across_sem, (step,), {"ctx": other}))
+
+    key_copy.wait_recv()
+    value_copy.wait_recv()
+    key_cube = cube_rows(keys[...], 1.0 / CUBE)
+    value_cube = cube_rows(values[...], 1.0 / CUBE)
+    for step in range(1, n_clip):
+        pass_on(step)
+
+    for head in range(heads):
+        at = slice(head * HD, (head + 1) * HD)
+        scores = dot_nt(query[:, at], keys[:, at]) * scaling
+        scores = jnp.where(allowed, scores, LOW)
+        expons = jnp.exp(scores - jnp.max(scores, axis=-1, keepdims=True))
+        fine_p = expons / jnp.sum(expons, axis=-1, keepdims=True)
+        fine[head] = fine_p
+        coarse_scores = dot_nt(query_cube[:, at], key_cube[:, at]) * scaling
+        coarse_scores = jnp.where(real, coarse_scores, LOW)
+        expons = jnp.exp(coarse_scores - jnp.max(coarse_scores, axis=-1, keepdims=True))
+        coarse_p = expons / jnp.sum(expons, axis=-1, keepdims=True)
+        coarse[head] = coarse_p
+        coarse_out = dot_nn(coarse_p.astype(jnp.bfloat16), value_cube[:, at])
+        fine_out = dot_nn(fine_p.astype(jnp.bfloat16), values[:, at])
+        result = (fine_out + over_tokens(coarse_out, cubes)).astype(jnp.bfloat16)
+        attention[:, at] = result
+        turned[at, slot(x, z)] = result.astype(jnp.float32).T.astype(jnp.bfloat16)
+
+    own_slot = turned.at[:, slot(x, z)]
+    turn_far = [send(own_slot, own_slot, turn_far_sem, (0,), {"ctx": other})]
+
+    weight_copy.wait()
+    layer_copy.wait()
+    parts = [None]
+    for step in range(1, n_clip):
+        clip = from_clip(step)
+        for copy in shares[step]:
+            copy.wait_recv()
+        partial[step] = dot_nt(columns[x, clip], held_weight[...]).astype(jnp.bfloat16)
+        parts.append(
+            send(
+                partial.at[step], partial_in.at[step], part_sem, (step,),
+                {"clip": clip},
+            )
+        )
+    turns = [None]
+    for step in range(1, n_clip):
+        turns.append(send(own_slot, own_slot, turn_sem, (step,), to_clip(step)))
+    total = dot_nt(columns[x, z], held_weight[...])
+    for copy in across:
+        copy.wait_recv()
+    far = columns.at[other, :, my_rows]
+    share_far = [
+        send(far, far, share_far_sem, (turn,), to_head(turn)) for turn in range(1, n_head)
+    ]
+    for step in range(1, n_clip):
+        parts[step].wait_recv()
+        total = total + partial_in[step].astype(jnp.float32)
+    grad[...] = total.astype(jnp.bfloat16)
+    grad_cube = cube_rows(grad[...], 1.0)
+
+    for head in range(heads):
+        at = slice(head * HD, (head + 1) * HD)
+        after = slice(width + head * HD, width + (head + 1) * HD)
+        fine_p = fine[head]
+        fine_half = fine_p.astype(jnp.bfloat16)
+        fine_dp = dot_nt(grad[:, at], values[:, at])
+        delta = jnp.sum(fine_p * fine_dp, axis=-1, keepdims=True)
+        fine_ds = (scaling * fine_p * (fine_dp - delta)).astype(jnp.bfloat16)
+        coarse_p = coarse[head]
+        coarse_half = coarse_p.astype(jnp.bfloat16)
+        coarse_dp = dot_nt(grad_cube[:, at], value_cube[:, at])
+        delta = jnp.sum(coarse_p * coarse_dp, axis=-1, keepdims=True)
+        coarse_ds = (scaling * coarse_p * (coarse_dp - delta)).astype(jnp.bfloat16)
+        coarse_dq = dot_nn(coarse_ds, key_cube[:, at]) * (1.0 / CUBE)
+        coarse_dk = dot_tn(coarse_ds, query_cube[:, at]) * (1.0 / CUBE)
+        coarse_dv = dot_tn(coarse_half, grad_cube[:, at]) * (1.0 / CUBE)
+        dq = dot_nn(fine_ds, keys[:, at]) + over_tokens(coarse_dq, cubes)
+        query_grad[:, at] = dq.astype(jnp.bfloat16)
+        dk = dot_tn(fine_ds, query[:, at]) + over_tokens(coarse_dk, cubes_whole)
+        dv = dot_tn(fine_half, grad[:, at]) + over_tokens(coarse_dv, cubes_whole)
+        dk, dv = dk.astype(jnp.bfloat16), dv.astype(jnp.bfloat16)
+        for ctx in range(2):
+            terms[ctx, :, at] = dk[ctx * tokens : (ctx + 1) * tokens]
+            terms[ctx, :, after] = dv[ctx * tokens : (ctx + 1) * tokens]
+
+    term_copy = send(terms.at[other], terms_in, term_sem, (), {"ctx": other})
+
+    for step in range(1, n_clip):
+        turns[step].wait_recv()
+        arrived = turned.at[:, slot(x, from_clip(step))]
+        turn_far.append(send(arrived, arrived, turn_far_sem, (step,), {"ctx": other}))
+    for copy in share_far + turn_far:
+        copy.wait_recv()
+    tile = 256
+    for begin in range(0, cols, tile):
+        block = columns[:, :, :, begin : begin + tile].reshape(2 * n_clip * tokens, tile)
+        weight_grad[:, begin : begin + tile] = dot_nn(turned[...], block).astype(jnp.bfloat16)
+
+    term_copy.wait_recv()
+    summed = terms[x].astype(jnp.float32) + terms_in[...].astype(jnp.float32)
+    key_grad[...] = summed[:, :width].astype(jnp.bfloat16)
+    value_grad[...] = summed[:, width:].astype(jnp.bfloat16)
+    for copy in sent:
+        copy.wait_send()
+
+
+def paired(n_clip, n_head, queries, key_states, value_states, layer_grad, out_weight, chosen):
+    tokens, width = queries.shape[1:]
+    cols = out_weight.shape[1]
+    heads = width // HD
+    half = jnp.bfloat16
+    whole = 2 * tokens
+    vmem = pl.BlockSpec(memory_space=pltpu.VMEM)
+    anywhere = pl.BlockSpec(memory_space=pl.ANY)
+    small = jax.ShapeDtypeStruct((tokens, width), half)
+    dma = pltpu.SemaphoreType.DMA
+    outs = pl.pallas_call(
+        functools.partial(pair_kernel, n_clip, n_head),
+        out_shape=(small, small, small, small, jax.ShapeDtypeStruct((width, cols), half)),
+        in_specs=[pl.BlockSpec(memory_space=pltpu.SMEM), vmem, vmem, vmem, anywhere, anywhere],
+        out_specs=(vmem,) * 5,
+        scratch_shapes=[
+            pltpu.VMEM((whole, width), half),
+            pltpu.VMEM((whole, width), half),
+            pltpu.VMEM((2, n_clip, tokens, cols), half),
+            pltpu.VMEM((width, cols), half),
+            pltpu.VMEM((heads, tokens, whole), jnp.float32),
+            pltpu.VMEM((heads, ROWS, ROWS), jnp.float32),
+            pltpu.VMEM((width, 2 * n_clip * tokens), half),
+            pltpu.VMEM((n_clip, tokens, width), half),
+            pltpu.VMEM((n_clip, tokens, width), half),
+            pltpu.VMEM((tokens, width), half),
+            pltpu.VMEM((2, tokens, 2 * width), half),
+            pltpu.VMEM((tokens, 2 * width), half),
+            dma((2, 2)),
+            dma((2, n_clip)),
+            dma((2, n_clip, n_head)),
+            dma((2, n_clip)),
+            dma((2, n_head)),
+            dma((2, n_clip)),
+            dma((2, n_clip)),
+            dma((2, n_clip)),
+            dma((2,)),
+            dma((2,)),
+        ],
+        compiler_params=pltpu.CompilerParams(
+            collective_id=0, has_side_effects=True, vmem_limit_bytes=40 * 2**20
+        ),
+    )(chosen[0], queries[0], key_states[0], value_states[0], layer_grad[0], out_weight)
+    return tuple(out[None] for out in outs[:4]) + (outs[4],)
+
 
 def solution(mesh):
+    clips, heads = mesh.shape["clip"], mesh.shape["head"]
+    paired_here = mesh.shape["ctx"] == 2
+    body = functools.partial(paired, clips, heads) if paired_here else on_device
     placed = (
         P("clip", "ctx", "head"),
         P("clip", "ctx", "head"),
@@ -156,7 +446,7 @@
         P("clip", "ctx", None),
     )
     return jax.shard_map(
-        on_device,
+        body,
         mesh=mesh,
         in_specs=placed,
         out_specs=(

time: 203 us -> 79.6 us (0.39)
  waiting for transfers between devices: 123 us -> 0 us
  Pallas kernels: 0 us -> 68.6 us
  matrix products: 16.4 us -> 0 us
  between operations: 14 us -> 0.66 us
  local copies, waits for them, and re-layouts: 20.2 us -> 9.99 us
  starting transfers between devices: 10.2 us -> 0 us
  blocking collectives: 9.85 us -> 0 us
  other arithmetic: 8.44 us -> 0 us
    all_gather x2 -> x0, waiting for transfers between devices: 83.4 us -> none  [the longest x1 44.4 us: on_device(): lax.all_gather(attention, ('ctx', 'clip'), axis=0, tiled=True)]
    pallas_call x0 -> x1, Pallas kernels: none -> 68.6 us  [paired(): pl.pallas_call(functools.partial(pair_kernel, n_clip, n_head), out_shape=...]
    all_to_all x2 -> x0, waiting for transfers between devices: 29.9 us -> none  [the longest x1 19.4 us: on_device(): lax.all_to_all(layer_local, 'clip', split_axis=1, concat_axis=0, tiled=True)]
    dot_general x13 -> x0, matrix products: 16.1 us -> none  [the longest x1 5.21 us: on_device(): lax.dot_general(attention_whole, columns_whole, (((0,), (0,)), ((), ())),...]
    all_to_all x2 -> x0, starting transfers between devices: 10.1 us -> none  [the longest x1 6.45 us: on_device(): lax.all_to_all(layer_local, 'clip', split_axis=1, concat_axis=0, tiled=True)]
    all_gather x1 -> x0, blocking collectives: 9.85 us -> none  [on_device(): lax.all_gather(jnp.concatenate([key_local, value_local], axis=1), 'ctx',...]
    reduce_scatter x1 -> x0, waiting for transfers between devices: 8.95 us -> none  [on_device(): lax.psum_scatter(running.reshape(tok_whole, 2 * width).astype(jnp.bfloat1...]
    unnamed x26 -> x17, local copies, waits for them, and re-layouts: 5.12 us -> 9.99 us
  transfers between devices with their start and end apart: 5 -> 0, of which waited for: 5 -> 0; matrix products, arithmetic and copies ran while one was open for 8% -> 0% of each run, Pallas kernels for 0% -> 0%
where the time goes in v2:
time: 79.6 us; the launch traced here: 79.3 us
  Pallas kernels  68.6 us (86%)
  local copies, waits for them, and re-layouts  9.99 us (13%)
    pallas_call x1, Pallas kernels, paired(): pl.pallas_call(functools.partial(pair_kernel, n_clip, n_head), out_shape=...  68.6 us
    unnamed x17, local copies, waits for them, and re-layouts  9.99 us

profile of v2, /device:TPU:0, one launch (start us, length us, event | category | flops | bytes accessed | tf_op | source)
XLA Modules:
  0.0 79.3 jit_solution(3076442718224123477)
XLA Ops:
  0.6 0.0 copy-start
  0.6 1.4 %copy-done = bf16[640,1280]{1,0:T(8,128)(2,1)S(1)} copy-done((bf16[640,1280]{1,0:T(8,128)(2,1)S(1)}, bf16[640,1280]{1,0:T(8,128)(2,1)}, u32[]{:S(2)}) %copy-start) | copy-done | bytes 1638424
  2.1 0.0 copy-start.1
  2.1 1.3 %copy-done.1 = bf16[1,128,5120]{2,1,0:T(8,128)(2,1)S(1)} copy-done((bf16[1,128,5120]{2,1,0:T(8,128)(2,1)S(1)}, bf16[1,128,5120]{2,1,0:T(8,128)(2,1)}, u32[]{:S(2)}) %copy-start.1) | copy-done | bytes 1310744
  3.4 0.0 copy-start.2
  3.4 0.9 %copy-done.2 = bf16[1,128,640]{2,1,0:T(8,128)(2,1)S(1)} copy-done((bf16[1,128,640]{2,1,0:T(8,128)(2,1)S(1)}, bf16[1,128,640]{2,1,0:T(8,128)(2,1)}, u32[]{:S(2)}) %copy-start.2) | copy-done | bytes 163864
  4.3 0.0 copy-start.3
  4.3 0.9 %copy-done.3 = bf16[1,128,640]{2,1,0:T(8,128)(2,1)S(1)} copy-done((bf16[1,128,640]{2,1,0:T(8,128)(2,1)S(1)}, bf16[1,128,640]{2,1,0:T(8,128)(2,1)}, u32[]{:S(2)}) %copy-start.3) | copy-done | bytes 163864
  5.2 0.0 copy-start.4
  5.2 0.9 %copy-done.4 = bf16[1,128,640]{2,1,0:T(8,128)(2,1)S(1)} copy-done((bf16[1,128,640]{2,1,0:T(8,128)(2,1)S(1)}, bf16[1,128,640]{2,1,0:T(8,128)(2,1)}, u32[]{:S(2)}) %copy-start.4) | copy-done | bytes 163864
  6.1 0.0 copy-start.5
  6.1 0.7 copy-done.5
  6.8 68.6 %shard_map.101 = (bf16[128,640]{1,0:T(8,128)(2,1)S(1)}, bf16[128,640]{1,0:T(8,128)(2,1)S(1)}, bf16[128,640]{1,0:T(8,128)(2,1)S(1)}, bf16[128,640]{1,0:T(8,128)(2,1)S(1)}, bf16[640,1280]{1,0:T(8,128)(2,1)S(1)}) custom-call(s32[2,2]{1,0:T(2,128)S(1)} %bitcast.17, bf16[128,640]{1,0:T(8,128)(2,1)S(1)} %bitcast.10, bf16[128,640]{1,0:T(8,128)(2,1)S(1)} %bitcast.11, ...), custom_call_target="tpu_custom_call" | custom-call | tf_op jit(solution)/shard_map/pallas_call | solution.py:400
  75.5 0.7 copy.16
  76.1 0.7 copy.17
  76.8 0.7 copy.18
  77.5 0.7 copy.19
  78.1 1.2 %copy.20 = bf16[640,1280]{1,0:T(8,128)(2,1)} copy(bf16[640,1280]{1,0:T(8,128)(2,1)S(1)} %get-tuple-element.24) | data formatting | bytes 3276800
Async XLA Ops:
  0.6 1.4 %copy-start = (bf16[640,1280]{1,0:T(8,128)(2,1)S(1)}, bf16[640,1280]{1,0:T(8,128)(2,1)}, u32[]{:S(2)}) copy-start(bf16[640,1280]{1,0:T(8,128)(2,1)} %weight.1) | copy-start | bytes 4915204
  2.1 1.3 %copy-start.1 = (bf16[1,128,5120]{2,1,0:T(8,128)(2,1)S(1)}, bf16[1,128,5120]{2,1,0:T(8,128)(2,1)}, u32[]{:S(2)}) copy-start(bf16[1,128,5120]{2,1,0:T(8,128)(2,1)} %param.9) | copy-start | bytes 3932164
  3.4 0.9 %copy-start.2 = (bf16[1,128,640]{2,1,0:T(8,128)(2,1)S(1)}, bf16[1,128,640]{2,1,0:T(8,128)(2,1)}, u32[]{:S(2)}) copy-start(bf16[1,128,640]{2,1,0:T(8,128)(2,1)} %param.6) | copy-start | bytes 491524
  4.3 0.9 %copy-start.3 = (bf16[1,128,640]{2,1,0:T(8,128)(2,1)S(1)}, bf16[1,128,640]{2,1,0:T(8,128)(2,1)}, u32[]{:S(2)}) copy-start(bf16[1,128,640]{2,1,0:T(8,128)(2,1)} %param.7) | copy-start | bytes 491524
  5.2 0.9 %copy-start.4 = (bf16[1,128,640]{2,1,0:T(8,128)(2,1)S(1)}, bf16[1,128,640]{2,1,0:T(8,128)(2,1)}, u32[]{:S(2)}) copy-start(bf16[1,128,640]{2,1,0:T(8,128)(2,1)} %param.8) | copy-start | bytes 491524
  6.1 0.7 copy-start.5

commit v3 on v2

--- a/solution.py
+++ b/solution.py
@@ -183,15 +183,15 @@
 
 
 def pair_kernel(
-    n_clip, n_head, chosen, query, key, value, layer, weight,
-    attention, query_grad, key_grad, value_grad, weight_grad,
-    keys, values, columns, held_weight, fine, coarse, turned,
+    n_clip, n_head, chosen_in, query_in, key, value, layer, weight,
+    attention_out, query_grad_out, key_grad_out, value_grad_out, weight_grad_out,
+    attention, query_grad, key_grad, value_grad, weight_grad, chosen, query, keys, values, columns, held_weight, weight_t, fine, coarse, turned,
     partial, partial_in, grad, terms, terms_in,
     kv_sem, deal_sem, share_sem, across_sem, share_far_sem, part_sem, turn_sem, turn_far_sem,
-    term_sem, local_sem,
+    term_sem, local_sem, out_sem,
 ):
     scaling = HD ** (-0.5)
-    tokens, width = query.shape
+    tokens, width = query_in.shape
     cols = weight.shape[1]
     heads = width // HD
     cubes = tokens // CUBE
@@ -216,7 +216,12 @@
     def slot(ctx, clip):
         return pl.ds(pl.multiple_of((ctx * n_clip + clip) * tokens, tokens), tokens)
 
-    sent = []
+    sent, written = [], []
+
+    def write(src, dst):
+        copy = pltpu.make_async_copy(src, dst, out_sem.at[len(written)])
+        copy.start()
+        written.append(copy)
 
     def send(src, dst, sems, index, device):
         copy = pltpu.make_async_remote_copy(
@@ -228,12 +233,22 @@
         sent.append(copy)
         return copy
 
-    weight_copy = pltpu.make_async_copy(weight, held_weight, local_sem.at[0])
-    weight_copy.start()
-    layer_copy = pltpu.make_async_copy(
-        layer.at[:, column_block(z)], columns.at[x, z], local_sem.at[1]
-    )
-    layer_copy.start()
+    mine = pl.ds(pl.multiple_of(x * tokens, tokens), tokens)
+    locals_in = [
+        pltpu.make_async_copy(src, dst, local_sem.at[index])
+        for index, (src, dst) in enumerate(
+            [
+                (query_in, query),
+                (key, keys.at[mine]),
+                (value, values.at[mine]),
+                (weight, held_weight),
+                (layer.at[:, column_block(z)], columns.at[x, z]),
+                (chosen_in, chosen),
+            ]
+        )
+    ]
+    for copy in locals_in:
+        copy.start()
 
     barrier = pltpu.get_barrier_semaphore()
     partners = [{"ctx": other}]
@@ -243,7 +258,6 @@
         pl.semaphore_signal(barrier, inc=1, device_id=partner, device_id_type=pl.DeviceIdType.MESH)
     pl.semaphore_wait(barrier, len(partners))
 
-    mine = pl.ds(pl.multiple_of(x * tokens, tokens), tokens)
     key_copy = send(key, keys.at[mine], kv_sem, (0,), {"ctx": other})
     value_copy = send(value, values.at[mine], kv_sem, (1,), {"ctx": other})
     deals = [None]
@@ -260,8 +274,11 @@
             across_sem, (0,), {"ctx": other},
         )
     ]
-    keys[mine, :] = key[...]
-    values[mine, :] = value[...]
+    for copy in locals_in:
+        copy.wait()
+    for head in range(heads):
+        at = slice(head * HD, (head + 1) * HD)
+        weight_t[:, at] = held_weight[at, :].T
     query_cube = cube_rows(query[...], 1.0 / CUBE)
     column_cube = lax.broadcasted_iota(jnp.int32, (1, cubes_whole * CUBE), 1) // CUBE
     allowed = []
@@ -289,6 +306,20 @@
     value_cube = cube_rows(values[...], 1.0 / CUBE)
     for step in range(1, n_clip):
         pass_on(step)
+
+    early = (heads + 1) // 2
+    split = (slice(0, early * HD), slice(early * HD, width))
+    turns, turn_far = [], []
+
+    def turn_out(part):
+        piece = turned.at[split[part], slot(x, z)]
+        turns.append(
+            [send(piece, piece, turn_sem, (part, step), to_clip(step)) for step in range(1, n_clip)]
+        )
+
+    def turn_across(part, step):
+        piece = turned.at[split[part], slot(x, from_clip(step))]
+        turn_far.append(send(piece, piece, turn_far_sem, (part, step), {"ctx": other}))
 
     for head in range(heads):
         at = slice(head * HD, (head + 1) * HD)
@@ -307,28 +338,25 @@
         result = (fine_out + over_tokens(coarse_out, cubes)).astype(jnp.bfloat16)
         attention[:, at] = result
         turned[at, slot(x, z)] = result.astype(jnp.float32).T.astype(jnp.bfloat16)
-
-    own_slot = turned.at[:, slot(x, z)]
-    turn_far = [send(own_slot, own_slot, turn_far_sem, (0,), {"ctx": other})]
-
-    weight_copy.wait()
-    layer_copy.wait()
+        if head == early - 1:
+            turn_out(0)
+            turn_across(0, 0)
+    turn_across(1, 0)
+    write(attention, attention_out)
+
     parts = [None]
     for step in range(1, n_clip):
         clip = from_clip(step)
         for copy in shares[step]:
             copy.wait_recv()
-        partial[step] = dot_nt(columns[x, clip], held_weight[...]).astype(jnp.bfloat16)
+        partial[step] = dot_nn(columns[x, clip], weight_t[...]).astype(jnp.bfloat16)
         parts.append(
             send(
                 partial.at[step], partial_in.at[step], part_sem, (step,),
                 {"clip": clip},
             )
         )
-    turns = [None]
-    for step in range(1, n_clip):
-        turns.append(send(own_slot, own_slot, turn_sem, (step,), to_clip(step)))
-    total = dot_nt(columns[x, z], held_weight[...])
+    total = dot_nn(columns[x, z], weight_t[...])
     for copy in across:
         copy.wait_recv()
     far = columns.at[other, :, my_rows]
@@ -336,8 +364,12 @@
         send(far, far, share_far_sem, (turn,), to_head(turn)) for turn in range(1, n_head)
     ]
     for step in range(1, n_clip):
+        turns[0][step - 1].wait_recv()
+        turn_across(0, step)
+    for step in range(1, n_clip):
         parts[step].wait_recv()
         total = total + partial_in[step].astype(jnp.float32)
+    turn_out(1)
     grad[...] = total.astype(jnp.bfloat16)
     grad_cube = cube_rows(grad[...], 1.0)
 
@@ -366,25 +398,42 @@
             terms[ctx, :, at] = dk[ctx * tokens : (ctx + 1) * tokens]
             terms[ctx, :, after] = dv[ctx * tokens : (ctx + 1) * tokens]
 
+    write(query_grad, query_grad_out)
     term_copy = send(terms.at[other], terms_in, term_sem, (), {"ctx": other})
 
     for step in range(1, n_clip):
-        turns[step].wait_recv()
-        arrived = turned.at[:, slot(x, from_clip(step))]
-        turn_far.append(send(arrived, arrived, turn_far_sem, (step,), {"ctx": other}))
+        turns[1][step - 1].wait_recv()
+        turn_across(1, step)
     for copy in share_far + turn_far:
         copy.wait_recv()
     tile = 256
     for begin in range(0, cols, tile):
         block = columns[:, :, :, begin : begin + tile].reshape(2 * n_clip * tokens, tile)
         weight_grad[:, begin : begin + tile] = dot_nn(turned[...], block).astype(jnp.bfloat16)
+        tile_at = slice(begin, begin + tile)
+        write(weight_grad.at[:, tile_at], weight_grad_out.at[:, tile_at])
 
     term_copy.wait_recv()
     summed = terms[x].astype(jnp.float32) + terms_in[...].astype(jnp.float32)
     key_grad[...] = summed[:, :width].astype(jnp.bfloat16)
     value_grad[...] = summed[:, width:].astype(jnp.bfloat16)
+    write(key_grad, key_grad_out)
+    write(value_grad, value_grad_out)
     for copy in sent:
         copy.wait_send()
+    for copy in written:
+        copy.wait()
+
+
+def copy_out(*refs):
+    sem = refs[-1]
+    copies = [
+        pltpu.make_async_copy(refs[index], refs[5 + index], sem.at[index]) for index in range(5)
+    ]
+    for copy in copies:
+        copy.start()
+    for copy in copies:
+        copy.wait()
 
 
 def paired(n_clip, n_head, queries, key_states, value_states, layer_grad, out_weight, chosen):
@@ -393,20 +442,24 @@
     heads = width // HD
     half = jnp.bfloat16
     whole = 2 * tokens
-    vmem = pl.BlockSpec(memory_space=pltpu.VMEM)
-    anywhere = pl.BlockSpec(memory_space=pl.ANY)
+    far = pl.BlockSpec(memory_space=pltpu.HBM)
     small = jax.ShapeDtypeStruct((tokens, width), half)
     dma = pltpu.SemaphoreType.DMA
     outs = pl.pallas_call(
         functools.partial(pair_kernel, n_clip, n_head),
         out_shape=(small, small, small, small, jax.ShapeDtypeStruct((width, cols), half)),
-        in_specs=[pl.BlockSpec(memory_space=pltpu.SMEM), vmem, vmem, vmem, anywhere, anywhere],
-        out_specs=(vmem,) * 5,
-        scratch_shapes=[
+        in_specs=[far] * 6,
+        out_specs=(far,) * 5,
+        scratch_shapes=[pltpu.VMEM((tokens, width), half)] * 4
+        + [
+            pltpu.VMEM((width, cols), half),
+            pltpu.SMEM(chosen.shape[1:], jnp.int32),
+            pltpu.VMEM((tokens, width), half),
             pltpu.VMEM((whole, width), half),
             pltpu.VMEM((whole, width), half),
             pltpu.VMEM((2, n_clip, tokens, cols), half),
             pltpu.VMEM((width, cols), half),
+            pltpu.VMEM((cols, width), half),
             pltpu.VMEM((heads, tokens, whole), jnp.float32),
             pltpu.VMEM((heads, ROWS, ROWS), jnp.float32),
             pltpu.VMEM((width, 2 * n_clip * tokens), half),
@@ -421,15 +474,24 @@
             dma((2, n_clip)),
             dma((2, n_head)),
             dma((2, n_clip)),
-            dma((2, n_clip)),
-            dma((2, n_clip)),
+            dma((2, 2, n_clip)),
+            dma((2, 2, n_clip)),
             dma((2,)),
-            dma((2,)),
+            dma((6,)),
+            dma((4 + cols // 256,)),
         ],
         compiler_params=pltpu.CompilerParams(
-            collective_id=0, has_side_effects=True, vmem_limit_bytes=40 * 2**20
+            collective_id=0, has_side_effects=True, vmem_limit_bytes=60 * 2**20
         ),
     )(chosen[0], queries[0], key_states[0], value_states[0], layer_grad[0], out_weight)
+    outs = pl.pallas_call(
+        copy_out,
+        out_shape=tuple(jax.ShapeDtypeStruct(out.shape, half) for out in outs),
+        in_specs=[far] * 5,
+        out_specs=(far,) * 5,
+        scratch_shapes=[dma((5,))],
+        compiler_params=pltpu.CompilerParams(vmem_limit_bytes=60 * 2**20),
+    )(*outs)
     return tuple(out[None] for out in outs[:4]) + (outs[4],)
 
 

time: 79.6 us -> 130 us (1.63)
  Pallas kernels: 68.6 us -> 129 us
  local copies, waits for them, and re-layouts: 9.99 us -> 0 us
    pallas_call x0 -> x1, Pallas kernels: none -> 70.6 us  [paired(): pl.pallas_call(copy_out, out_shape=tuple((jax.ShapeDtypeStruct(out.shape,...]
    pallas_call x1, Pallas kernels: 68.6 us -> 58.4 us  [paired(): pl.pallas_call(functools.partial(pair_kernel, n_clip, n_head), out_shape=...]
    unnamed x17 -> x0, local copies, waits for them, and re-layouts: 9.99 us -> none
where the time goes in v3:
time: 130 us
  Pallas kernels  129 us (99%)
    pallas_call x1, Pallas kernels, paired(): pl.pallas_call(copy_out, out_shape=tuple((jax.ShapeDtypeStruct(out.shape,...  70.6 us
    pallas_call x1, Pallas kernels, paired(): pl.pallas_call(functools.partial(pair_kernel, n_clip, n_head), out_shape=...  58.4 us

profile of v3, /device:TPU:0, one launch (start us, length us, event | category | flops | bytes accessed | tf_op | source)
XLA Modules:
  0.0 129.7 jit_solution(15235504903432338218)
XLA Ops:
  0.6 58.4 %shard_map.101 = (bf16[128,640]{1,0:T(8,128)(2,1)}, bf16[128,640]{1,0:T(8,128)(2,1)}, bf16[128,640]{1,0:T(8,128)(2,1)}, bf16[128,640]{1,0:T(8,128)(2,1)}, bf16[640,1280]{1,0:T(8,128)(2,1)}) custom-call(s32[2,2]{1,0:T(2,128)} %bitcast.13, bf16[128,640]{1,0:T(8,128)(2,1)} %bitcast.10, bf16[128,640]{1,0:T(8,128)(2,1)} %bitcast.11, bf16[128,640]{1,0:T(8,128)(2,1)} %bitcast.12, ...), custom_call_target="tpu_custom_call" | custom-call | tf_op jit(solution)/shard_map/pallas_call | solution.py:448
  59.0 70.6 %shard_map.102 = (bf16[128,640]{1,0:T(8,128)(2,1)}, bf16[128,640]{1,0:T(8,128)(2,1)}, bf16[128,640]{1,0:T(8,128)(2,1)}, bf16[128,640]{1,0:T(8,128)(2,1)}, bf16[640,1280]{1,0:T(8,128)(2,1)}) custom-call(bf16[128,640]{1,0:T(8,128)(2,1)} %get-tuple-element.15.refs_0_, bf16[128,640]{1,0:T(8,128)(2,1)} %get-tuple-element.16.refs_1_, ...), custom_call_target="tpu_custom_call" | custom-call | tf_op jit(solution)/shard_map/pallas_call | solution.py:487

commit v4 on v3

--- a/solution.py
+++ b/solution.py
@@ -199,16 +199,18 @@
     quarter = tokens // n_head
     x, h, z = lax.axis_index("ctx"), lax.axis_index("head"), lax.axis_index("clip")
     other = 1 - x
-    my_rows = pl.ds(pl.multiple_of(h * quarter, quarter), quarter)
+    near, over = h + 1 - 2 * lax.rem(h, 2), lax.rem(h + 2, n_head)
+
+    def rows_of(head):
+        return pl.ds(pl.multiple_of(head * quarter, quarter), quarter)
+
+    my_rows, over_rows = rows_of(h), rows_of(over)
 
     def to_clip(step):
         return {"clip": lax.rem(z + step, n_clip)}
 
     def from_clip(step):
         return lax.rem(z + n_clip - step, n_clip)
-
-    def to_head(step):
-        return {"head": lax.rem(h + step, n_head)}
 
     def column_block(clip):
         return pl.ds(pl.multiple_of(clip * cols, cols), cols)
@@ -253,7 +255,7 @@
     barrier = pltpu.get_barrier_semaphore()
     partners = [{"ctx": other}]
     partners += [to_clip(step) for step in range(1, n_clip)]
-    partners += [to_head(step) for step in range(1, n_head)]
+    partners += [{"head": near}, {"head": over}]
     for partner in partners:
         pl.semaphore_signal(barrier, inc=1, device_id=partner, device_id_type=pl.DeviceIdType.MESH)
     pl.semaphore_wait(barrier, len(partners))
@@ -296,7 +298,10 @@
         deals[step].wait_recv()
         piece = columns.at[x, from_clip(step), my_rows]
         shares.append(
-            [send(piece, piece, share_sem, (step, turn), to_head(turn)) for turn in range(1, n_head)]
+            [
+                send(piece, piece, share_sem, (step, 0), {"head": over}),
+                send(piece, piece, share_sem, (step, 1), {"head": near}),
+            ]
         )
         across.append(send(piece, piece, across_sem, (step,), {"ctx": other}))
 
@@ -344,10 +349,14 @@
     turn_across(1, 0)
     write(attention, attention_out)
 
+    for step in range(1, n_clip):
+        shares[step][0].wait_recv()
+        piece = columns.at[x, from_clip(step), over_rows]
+        shares[step].append(send(piece, piece, share_sem, (step, 2), {"head": near}))
     parts = [None]
     for step in range(1, n_clip):
         clip = from_clip(step)
-        for copy in shares[step]:
+        for copy in shares[step][1:]:
             copy.wait_recv()
         partial[step] = dot_nn(columns[x, clip], weight_t[...]).astype(jnp.bfloat16)
         parts.append(
@@ -361,11 +370,27 @@
         copy.wait_recv()
     far = columns.at[other, :, my_rows]
     share_far = [
-        send(far, far, share_far_sem, (turn,), to_head(turn)) for turn in range(1, n_head)
+        send(far, far, share_far_sem, (0,), {"head": over}),
+        send(far, far, share_far_sem, (1,), {"head": near}),
     ]
     for step in range(1, n_clip):
         turns[0][step - 1].wait_recv()
         turn_across(0, step)
+    share_far[0].wait_recv()
+    far = columns.at[other, :, over_rows]
+    share_far.append(send(far, far, share_far_sem, (2,), {"head": near}))
+    for copy in share_far[1:] + turn_far[:1] + turn_far[2:]:
+        copy.wait_recv()
+
+    def weight_rows(part):
+        for begin in range(0, cols, tile):
+            at = slice(begin, begin + tile)
+            block = columns[:, :, :, at].reshape(2 * n_clip * tokens, tile)
+            weight_grad[split[part], at] = dot_nn(turned[split[part], :], block).astype(jnp.bfloat16)
+        write(weight_grad.at[split[part]], weight_grad_out.at[split[part]])
+
+    tile = 256
+    weight_rows(0)
     for step in range(1, n_clip):
         parts[step].wait_recv()
         total = total + partial_in[step].astype(jnp.float32)
@@ -373,9 +398,9 @@
     grad[...] = total.astype(jnp.bfloat16)
     grad_cube = cube_rows(grad[...], 1.0)
 
+    term_copies = []
     for head in range(heads):
         at = slice(head * HD, (head + 1) * HD)
-        after = slice(width + head * HD, width + (head + 1) * HD)
         fine_p = fine[head]
         fine_half = fine_p.astype(jnp.bfloat16)
         fine_dp = dot_nt(grad[:, at], values[:, at])
@@ -395,28 +420,27 @@
         dv = dot_tn(fine_half, grad[:, at]) + over_tokens(coarse_dv, cubes_whole)
         dk, dv = dk.astype(jnp.bfloat16), dv.astype(jnp.bfloat16)
         for ctx in range(2):
-            terms[ctx, :, at] = dk[ctx * tokens : (ctx + 1) * tokens]
-            terms[ctx, :, after] = dv[ctx * tokens : (ctx + 1) * tokens]
+            terms[ctx, head, 0] = dk[ctx * tokens : (ctx + 1) * tokens]
+            terms[ctx, head, 1] = dv[ctx * tokens : (ctx + 1) * tokens]
+        term_copies.append(
+            send(terms.at[other, head], terms_in.at[head], term_sem, (head,), {"ctx": other})
+        )
 
     write(query_grad, query_grad_out)
-    term_copy = send(terms.at[other], terms_in, term_sem, (), {"ctx": other})
 
     for step in range(1, n_clip):
         turns[1][step - 1].wait_recv()
         turn_across(1, step)
-    for copy in share_far + turn_far:
+    for copy in turn_far[1:2] + turn_far[-(n_clip - 1) :]:
         copy.wait_recv()
-    tile = 256
-    for begin in range(0, cols, tile):
-        block = columns[:, :, :, begin : begin + tile].reshape(2 * n_clip * tokens, tile)
-        weight_grad[:, begin : begin + tile] = dot_nn(turned[...], block).astype(jnp.bfloat16)
-        tile_at = slice(begin, begin + tile)
-        write(weight_grad.at[:, tile_at], weight_grad_out.at[:, tile_at])
-
-    term_copy.wait_recv()
-    summed = terms[x].astype(jnp.float32) + terms_in[...].astype(jnp.float32)
-    key_grad[...] = summed[:, :width].astype(jnp.bfloat16)
-    value_grad[...] = summed[:, width:].astype(jnp.bfloat16)
+    weight_rows(1)
+
+    for head in range(heads):
+        at = slice(head * HD, (head + 1) * HD)
+        term_copies[head].wait_recv()
+        summed = terms[x, head].astype(jnp.float32) + terms_in[head].astype(jnp.float32)
+        key_grad[:, at] = summed[0].astype(jnp.bfloat16)
+        value_grad[:, at] = summed[1].astype(jnp.bfloat16)
     write(key_grad, key_grad_out)
     write(value_grad, value_grad_out)
     for copy in sent:
@@ -427,12 +451,21 @@
 
 def copy_out(*refs):
     sem = refs[-1]
-    copies = [
-        pltpu.make_async_copy(refs[index], refs[5 + index], sem.at[index]) for index in range(5)
+    n_out = len(refs) // 3
+    loads = [
+        pltpu.make_async_copy(refs[index], refs[2 * n_out + index], sem.at[0, index])
+        for index in range(n_out)
     ]
-    for copy in copies:
+    stores = [
+        pltpu.make_async_copy(refs[2 * n_out + index], refs[n_out + index], sem.at[1, index])
+        for index in range(n_out)
+    ]
+    for copy in loads:
         copy.start()
-    for copy in copies:
+    for load, store in zip(loads, stores):
+        load.wait()
+        store.start()
+    for copy in stores:
         copy.wait()
 
 
@@ -466,8 +499,8 @@
             pltpu.VMEM((n_clip, tokens, width), half),
             pltpu.VMEM((n_clip, tokens, width), half),
             pltpu.VMEM((tokens, width), half),
-            pltpu.VMEM((2, tokens, 2 * width), half),
-            pltpu.VMEM((tokens, 2 * width), half),
+            pltpu.VMEM((2, heads, 2, tokens, HD), half),
+            pltpu.VMEM((heads, 2, tokens, HD), half),
             dma((2, 2)),
             dma((2, n_clip)),
             dma((2, n_clip, n_head)),
@@ -476,9 +509,9 @@
             dma((2, n_clip)),
             dma((2, 2, n_clip)),
             dma((2, 2, n_clip)),
-            dma((2,)),
+            dma((2, heads)),
             dma((6,)),
-            dma((4 + cols // 256,)),
+            dma((6,)),
         ],
         compiler_params=pltpu.CompilerParams(
             collective_id=0, has_side_effects=True, vmem_limit_bytes=60 * 2**20
@@ -489,7 +522,7 @@
         out_shape=tuple(jax.ShapeDtypeStruct(out.shape, half) for out in outs),
         in_specs=[far] * 5,
         out_specs=(far,) * 5,
-        scratch_shapes=[dma((5,))],
+        scratch_shapes=[pltpu.VMEM(out.shape, half) for out in outs] + [dma((2, 5))],
         compiler_params=pltpu.CompilerParams(vmem_limit_bytes=60 * 2**20),
     )(*outs)
     return tuple(out[None] for out in outs[:4]) + (outs[4],)
@@ -497,7 +530,7 @@
 
 def solution(mesh):
     clips, heads = mesh.shape["clip"], mesh.shape["head"]
-    paired_here = mesh.shape["ctx"] == 2
+    paired_here = mesh.shape["ctx"] == 2 and heads == 4
     body = functools.partial(paired, clips, heads) if paired_here else on_device
     placed = (
         P("clip", "ctx", "head"),

time: 130 us -> 57.6 us (0.44)
  Pallas kernels: 129 us -> 56.8 us
    pallas_call x1, Pallas kernels: 70.6 us -> 3.02 us  [paired(): pl.pallas_call(copy_out, out_shape=tuple((jax.ShapeDtypeStruct(out.shape,...]
    pallas_call x1, Pallas kernels: 58.4 us -> 53.8 us  [paired(): pl.pallas_call(functools.partial(pair_kernel, n_clip, n_head), out_shape=...]
where the time goes in v4:
time: 57.6 us; the launch traced here: 57.4 us
  Pallas kernels  56.8 us (99%)
  between operations  0.64 us (1%)
    pallas_call x1, Pallas kernels, paired(): pl.pallas_call(functools.partial(pair_kernel, n_clip, n_head), out_shape=...  53.8 us
    pallas_call x1, Pallas kernels, paired(): pl.pallas_call(copy_out, out_shape=tuple((jax.ShapeDtypeStruct(out.shape,...  3.02 us

profile of v4, /device:TPU:0, one launch (start us, length us, event | category | flops | bytes accessed | tf_op | source)
XLA Modules:
  0.0 57.4 jit_solution(3815286744191449587)
XLA Ops:
  0.6 53.8 %shard_map.101 = (bf16[128,640]{1,0:T(8,128)(2,1)}, bf16[128,640]{1,0:T(8,128)(2,1)}, bf16[128,640]{1,0:T(8,128)(2,1)}, bf16[128,640]{1,0:T(8,128)(2,1)}, bf16[640,1280]{1,0:T(8,128)(2,1)}) custom-call(s32[2,2]{1,0:T(2,128)} %bitcast.13, bf16[128,640]{1,0:T(8,128)(2,1)} %bitcast.10, bf16[128,640]{1,0:T(8,128)(2,1)} %bitcast.11, bf16[128,640]{1,0:T(8,128)(2,1)} %bitcast.12, ...), custom_call_target="tpu_custom_call" | custom-call | tf_op jit(solution)/shard_map/pallas_call | solution.py:481
  54.4 3.0 %shard_map.102 = (bf16[128,640]{1,0:T(8,128)(2,1)}, bf16[128,640]{1,0:T(8,128)(2,1)}, bf16[128,640]{1,0:T(8,128)(2,1)}, bf16[128,640]{1,0:T(8,128)(2,1)}, bf16[640,1280]{1,0:T(8,128)(2,1)}) custom-call(bf16[128,640]{1,0:T(8,128)(2,1)} %get-tuple-element.15.refs_0_, bf16[128,640]{1,0:T(8,128)(2,1)} %get-tuple-element.16.refs_1_, ...), custom_call_target="tpu_custom_call" | custom-call | tf_op jit(solution)/shard_map/pallas_call | solution.py:520

commit v5 on v4

--- a/solution.py
+++ b/solution.py
@@ -305,54 +305,58 @@
         )
         across.append(send(piece, piece, across_sem, (step,), {"ctx": other}))
 
+    def hand_on(step):
+        shares[step][0].wait_recv()
+        piece = columns.at[x, from_clip(step), over_rows]
+        shares[step].append(send(piece, piece, share_sem, (step, 2), {"head": near}))
+
     key_copy.wait_recv()
-    value_copy.wait_recv()
     key_cube = cube_rows(keys[...], 1.0 / CUBE)
-    value_cube = cube_rows(values[...], 1.0 / CUBE)
-    for step in range(1, n_clip):
-        pass_on(step)
-
-    early = (heads + 1) // 2
-    split = (slice(0, early * HD), slice(early * HD, width))
-    turns, turn_far = [], []
-
-    def turn_out(part):
-        piece = turned.at[split[part], slot(x, z)]
-        turns.append(
-            [send(piece, piece, turn_sem, (part, step), to_clip(step)) for step in range(1, n_clip)]
-        )
-
-    def turn_across(part, step):
-        piece = turned.at[split[part], slot(x, from_clip(step))]
-        turn_far.append(send(piece, piece, turn_far_sem, (part, step), {"ctx": other}))
-
     for head in range(heads):
         at = slice(head * HD, (head + 1) * HD)
         scores = dot_nt(query[:, at], keys[:, at]) * scaling
         scores = jnp.where(allowed, scores, LOW)
         expons = jnp.exp(scores - jnp.max(scores, axis=-1, keepdims=True))
-        fine_p = expons / jnp.sum(expons, axis=-1, keepdims=True)
-        fine[head] = fine_p
+        fine[head] = expons / jnp.sum(expons, axis=-1, keepdims=True)
         coarse_scores = dot_nt(query_cube[:, at], key_cube[:, at]) * scaling
         coarse_scores = jnp.where(real, coarse_scores, LOW)
         expons = jnp.exp(coarse_scores - jnp.max(coarse_scores, axis=-1, keepdims=True))
-        coarse_p = expons / jnp.sum(expons, axis=-1, keepdims=True)
-        coarse[head] = coarse_p
-        coarse_out = dot_nn(coarse_p.astype(jnp.bfloat16), value_cube[:, at])
-        fine_out = dot_nn(fine_p.astype(jnp.bfloat16), values[:, at])
+        coarse[head] = expons / jnp.sum(expons, axis=-1, keepdims=True)
+
+    for step in range(1, n_clip):
+        pass_on(step)
+    value_copy.wait_recv()
+    value_cube = cube_rows(values[...], 1.0 / CUBE)
+
+    early = (heads + 1) // 2
+    split = (slice(0, early * HD), slice(early * HD, width))
+    turns, turn_far = [], []
+
+    def turn_out(part):
+        piece = turned.at[split[part], slot(x, z)]
+        turns.append(
+            [send(piece, piece, turn_sem, (part, step), to_clip(step)) for step in range(1, n_clip)]
+        )
+
+    def turn_across(part, step):
+        piece = turned.at[split[part], slot(x, from_clip(step))]
+        turn_far.append(send(piece, piece, turn_far_sem, (part, step), {"ctx": other}))
+
+    for head in range(heads):
+        at = slice(head * HD, (head + 1) * HD)
+        coarse_out = dot_nn(coarse[head].astype(jnp.bfloat16), value_cube[:, at])
+        fine_out = dot_nn(fine[head].astype(jnp.bfloat16), values[:, at])
         result = (fine_out + over_tokens(coarse_out, cubes)).astype(jnp.bfloat16)
         attention[:, at] = result
         turned[at, slot(x, z)] = result.astype(jnp.float32).T.astype(jnp.bfloat16)
         if head == early - 1:
             turn_out(0)
             turn_across(0, 0)
+            for step in range(1, n_clip):
+                hand_on(step)
     turn_across(1, 0)
     write(attention, attention_out)
 
-    for step in range(1, n_clip):
-        shares[step][0].wait_recv()
-        piece = columns.at[x, from_clip(step), over_rows]
-        shares[step].append(send(piece, piece, share_sem, (step, 2), {"head": near}))
     parts = [None]
     for step in range(1, n_clip):
         clip = from_clip(step)
@@ -431,10 +435,6 @@
     for step in range(1, n_clip):
         turns[1][step - 1].wait_recv()
         turn_across(1, step)
-    for copy in turn_far[1:2] + turn_far[-(n_clip - 1) :]:
-        copy.wait_recv()
-    weight_rows(1)
-
     for head in range(heads):
         at = slice(head * HD, (head + 1) * HD)
         term_copies[head].wait_recv()
@@ -443,6 +443,9 @@
         value_grad[:, at] = summed[1].astype(jnp.bfloat16)
     write(key_grad, key_grad_out)
     write(value_grad, value_grad_out)
+    for copy in turn_far[1:2] + turn_far[-(n_clip - 1) :]:
+        copy.wait_recv()
+    weight_rows(1)
     for copy in sent:
         copy.wait_send()
     for copy in written:

time: 57.6 us -> 56.3 us (0.977)
  Pallas kernels: 56.8 us -> 55.5 us
    pallas_call x1, Pallas kernels: 53.8 us -> 52.5 us  [paired(): pl.pallas_call(functools.partial(pair_kernel, n_clip, n_head), out_shape=...]
where the time goes in v5:
time: 56.3 us; the launch traced here: 56.2 us
  Pallas kernels  55.5 us (99%)
  between operations  0.64 us (1%)
    pallas_call x1, Pallas kernels, paired(): pl.pallas_call(functools.partial(pair_kernel, n_clip, n_head), out_shape=...  52.5 us
    pallas_call x1, Pallas kernels, paired(): pl.pallas_call(copy_out, out_shape=tuple((jax.ShapeDtypeStruct(out.shape,...  3.02 us

profile of v5, /device:TPU:0, one launch (start us, length us, event | category | flops | bytes accessed | tf_op | source)
XLA Modules:
  0.0 56.2 jit_solution(11148368355908251085)
XLA Ops:
  0.6 52.5 %shard_map.101 = (bf16[128,640]{1,0:T(8,128)(2,1)}, bf16[128,640]{1,0:T(8,128)(2,1)}, bf16[128,640]{1,0:T(8,128)(2,1)}, bf16[128,640]{1,0:T(8,128)(2,1)}, bf16[640,1280]{1,0:T(8,128)(2,1)}) custom-call(s32[2,2]{1,0:T(2,128)} %bitcast.13, bf16[128,640]{1,0:T(8,128)(2,1)} %bitcast.10, bf16[128,640]{1,0:T(8,128)(2,1)} %bitcast.11, bf16[128,640]{1,0:T(8,128)(2,1)} %bitcast.12, ...), custom_call_target="tpu_custom_call" | custom-call | tf_op jit(solution)/shard_map/pallas_call | solution.py:484
  53.1 3.0 %shard_map.102 = (bf16[128,640]{1,0:T(8,128)(2,1)}, bf16[128,640]{1,0:T(8,128)(2,1)}, bf16[128,640]{1,0:T(8,128)(2,1)}, bf16[128,640]{1,0:T(8,128)(2,1)}, bf16[640,1280]{1,0:T(8,128)(2,1)}) custom-call(bf16[128,640]{1,0:T(8,128)(2,1)} %get-tuple-element.15.refs_0_, bf16[128,640]{1,0:T(8,128)(2,1)} %get-tuple-element.16.refs_1_, ...), custom_call_target="tpu_custom_call" | custom-call | tf_op jit(solution)/shard_map/pallas_call | solution.py:523

commit v6 on v5

--- a/solution.py
+++ b/solution.py
@@ -332,7 +332,40 @@
     split = (slice(0, early * HD), slice(early * HD, width))
     turns, turn_far = [], []
 
+    relayed = n_clip == 4
+    ends = (z == 0) | (z == n_clip - 1)
+    far_end = n_clip - 1 - lax.rem(z + 2, n_clip)
+
+    def end_to_end(step):
+        return ends & (lax.rem(z + step, n_clip) == n_clip - 1 - z)
+
+    def turn_relayed():
+        piece = turned.at[split[0], slot(x, z)]
+        copies = []
+        for step in range(1, n_clip):
+            copy = pltpu.make_async_remote_copy(
+                src_ref=piece, dst_ref=piece,
+                send_sem=turn_sem.at[0, 0, step], recv_sem=turn_sem.at[1, 0, step],
+                device_id=to_clip(step), device_id_type=pl.DeviceIdType.MESH,
+            )
+            pl.when(jnp.logical_not(end_to_end(step)))(copy.start)
+            copies.append(copy)
+        turns.append(copies)
+
+    def relay():
+        source = lax.rem(z + 2, n_clip)
+        piece = turned.at[split[0], slot(x, source)]
+        step = lax.rem(far_end - source + n_clip, n_clip)
+        return pltpu.make_async_remote_copy(
+            src_ref=piece, dst_ref=piece,
+            send_sem=turn_sem.at[0, 0, 0], recv_sem=turn_sem.at[1, 0, step],
+            device_id={"clip": far_end}, device_id_type=pl.DeviceIdType.MESH,
+        )
+
     def turn_out(part):
+        if part == 0 and relayed:
+            turn_relayed()
+            return
         piece = turned.at[split[part], slot(x, z)]
         turns.append(
             [send(piece, piece, turn_sem, (part, step), to_clip(step)) for step in range(1, n_clip)]
@@ -377,8 +410,10 @@
         send(far, far, share_far_sem, (0,), {"head": over}),
         send(far, far, share_far_sem, (1,), {"head": near}),
     ]
-    for step in range(1, n_clip):
+    for step in [2, 1, 3] if relayed else range(1, n_clip):
         turns[0][step - 1].wait_recv()
+        if relayed and step == 2:
+            pl.when(jnp.logical_not(ends))(lambda: relay().start())
         turn_across(0, step)
     share_far[0].wait_recv()
     far = columns.at[other, :, over_rows]
@@ -446,6 +481,10 @@
     for copy in turn_far[1:2] + turn_far[-(n_clip - 1) :]:
         copy.wait_recv()
     weight_rows(1)
+    if relayed:
+        for step in range(1, n_clip):
+            pl.when(jnp.logical_not(end_to_end(step)))(turns[0][step - 1].wait_send)
+        pl.when(jnp.logical_not(ends))(lambda: relay().wait_send())
     for copy in sent:
         copy.wait_send()
     for copy in written:

time: 56.3 us -> 56 us (level)
  Pallas kernels: 55.5 us -> 54.8 us
    pallas_call x1, Pallas kernels: 52.5 us -> 51.8 us  [paired(): pl.pallas_call(functools.partial(pair_kernel, n_clip, n_head), out_shape=...]
where the time goes in v6:
time: 56 us; the launch traced here: 55.4 us
  Pallas kernels  54.8 us (98%)
  between operations  0.64 us (1%)
    pallas_call x1, Pallas kernels, paired(): pl.pallas_call(functools.partial(pair_kernel, n_clip, n_head), out_shape=...  51.8 us
    pallas_call x1, Pallas kernels, paired(): pl.pallas_call(copy_out, out_shape=tuple((jax.ShapeDtypeStruct(out.shape,...  3.02 us

profile of v6, /device:TPU:0, one launch (start us, length us, event | category | flops | bytes accessed | tf_op | source)
XLA Modules:
  0.0 55.4 jit_solution(13504327620575255249)
XLA Ops:
  0.6 51.8 %shard_map.101 = (bf16[128,640]{1,0:T(8,128)(2,1)}, bf16[128,640]{1,0:T(8,128)(2,1)}, bf16[128,640]{1,0:T(8,128)(2,1)}, bf16[128,640]{1,0:T(8,128)(2,1)}, bf16[640,1280]{1,0:T(8,128)(2,1)}) custom-call(s32[2,2]{1,0:T(2,128)} %bitcast.13, bf16[128,640]{1,0:T(8,128)(2,1)} %bitcast.10, bf16[128,640]{1,0:T(8,128)(2,1)} %bitcast.11, bf16[128,640]{1,0:T(8,128)(2,1)} %bitcast.12, ...), custom_call_target="tpu_custom_call" | custom-call | tf_op jit(solution)/shard_map/pallas_call | solution.py:523
  52.4 3.0 %shard_map.102 = (bf16[128,640]{1,0:T(8,128)(2,1)}, bf16[128,640]{1,0:T(8,128)(2,1)}, bf16[128,640]{1,0:T(8,128)(2,1)}, bf16[128,640]{1,0:T(8,128)(2,1)}, bf16[640,1280]{1,0:T(8,128)(2,1)}) custom-call(bf16[128,640]{1,0:T(8,128)(2,1)} %get-tuple-element.15.refs_0_, bf16[128,640]{1,0:T(8,128)(2,1)} %get-tuple-element.16.refs_1_, ...), custom_call_target="tpu_custom_call" | custom-call | tf_op jit(solution)/shard_map/pallas_call | solution.py:562

commit v7 on v5

--- a/solution.py
+++ b/solution.py
@@ -328,7 +328,7 @@
     value_copy.wait_recv()
     value_cube = cube_rows(values[...], 1.0 / CUBE)
 
-    early = (heads + 1) // 2
+    early = heads - 1
     split = (slice(0, early * HD), slice(early * HD, width))
     turns, turn_far = [], []
 
@@ -352,6 +352,7 @@
         if head == early - 1:
             turn_out(0)
             turn_across(0, 0)
+        if head == heads // 2:
             for step in range(1, n_clip):
                 hand_on(step)
     turn_across(1, 0)
@@ -380,11 +381,6 @@
     for step in range(1, n_clip):
         turns[0][step - 1].wait_recv()
         turn_across(0, step)
-    share_far[0].wait_recv()
-    far = columns.at[other, :, over_rows]
-    share_far.append(send(far, far, share_far_sem, (2,), {"head": near}))
-    for copy in share_far[1:] + turn_far[:1] + turn_far[2:]:
-        copy.wait_recv()
 
     def weight_rows(part):
         for begin in range(0, cols, tile):
@@ -394,12 +390,14 @@
         write(weight_grad.at[split[part]], weight_grad_out.at[split[part]])
 
     tile = 256
-    weight_rows(0)
     for step in range(1, n_clip):
         parts[step].wait_recv()
         total = total + partial_in[step].astype(jnp.float32)
     turn_out(1)
     grad[...] = total.astype(jnp.bfloat16)
+    share_far[0].wait_recv()
+    far = columns.at[other, :, over_rows]
+    share_far.append(send(far, far, share_far_sem, (2,), {"head": near}))
     grad_cube = cube_rows(grad[...], 1.0)
 
     term_copies = []
@@ -431,10 +429,13 @@
         )
 
     write(query_grad, query_grad_out)
-
+    for copy in share_far[1:] + turn_far[:1] + turn_far[2:]:
+        copy.wait_recv()
     for step in range(1, n_clip):
         turns[1][step - 1].wait_recv()
         turn_across(1, step)
+    weight_rows(0)
+
     for head in range(heads):
         at = slice(head * HD, (head + 1) * HD)
         term_copies[head].wait_recv()

time: 56.3 us -> 59 us (1.048)
  Pallas kernels: 55.5 us -> 58.2 us
    pallas_call x1, Pallas kernels: 52.5 us -> 55.1 us  [paired(): pl.pallas_call(functools.partial(pair_kernel, n_clip, n_head), out_shape=...]
where the time goes in v7:
time: 59 us; the launch traced here: 58.8 us
  Pallas kernels  58.2 us (99%)
  between operations  0.64 us (1%)
    pallas_call x1, Pallas kernels, paired(): pl.pallas_call(functools.partial(pair_kernel, n_clip, n_head), out_shape=...  55.1 us
    pallas_call x1, Pallas kernels, paired(): pl.pallas_call(copy_out, out_shape=tuple((jax.ShapeDtypeStruct(out.shape,...  3.02 us

profile of v7, /device:TPU:0, one launch (start us, length us, event | category | flops | bytes accessed | tf_op | source)
XLA Modules:
  0.0 58.8 jit_solution(9051823465806184139)
XLA Ops:
  0.6 55.1 %shard_map.101 = (bf16[128,640]{1,0:T(8,128)(2,1)}, bf16[128,640]{1,0:T(8,128)(2,1)}, bf16[128,640]{1,0:T(8,128)(2,1)}, bf16[128,640]{1,0:T(8,128)(2,1)}, bf16[640,1280]{1,0:T(8,128)(2,1)}) custom-call(s32[2,2]{1,0:T(2,128)} %bitcast.13, bf16[128,640]{1,0:T(8,128)(2,1)} %bitcast.10, bf16[128,640]{1,0:T(8,128)(2,1)} %bitcast.11, bf16[128,640]{1,0:T(8,128)(2,1)} %bitcast.12, ...), custom_call_target="tpu_custom_call" | custom-call | tf_op jit(solution)/shard_map/pallas_call | solution.py:485
  55.8 3.0 %shard_map.102 = (bf16[128,640]{1,0:T(8,128)(2,1)}, bf16[128,640]{1,0:T(8,128)(2,1)}, bf16[128,640]{1,0:T(8,128)(2,1)}, bf16[128,640]{1,0:T(8,128)(2,1)}, bf16[640,1280]{1,0:T(8,128)(2,1)}) custom-call(bf16[128,640]{1,0:T(8,128)(2,1)} %get-tuple-element.15.refs_0_, bf16[128,640]{1,0:T(8,128)(2,1)} %get-tuple-element.16.refs_1_, ...), custom_call_target="tpu_custom_call" | custom-call | tf_op jit(solution)/shard_map/pallas_call | solution.py:524
